TPU v7x, 256 devices: a whole 4x4x8 slice. The times are simulated.
256 devices in a mesh: chan: 16 (over z, y_hi), patch: 16 (over x, y_lo, core).
Axes of the slice: x: 4, y: 4 (y_hi: 2, y_lo: 2; y = y_hi * 2 + y_lo), z: 8, core: 2. Of those that a mesh axis runs over, the one named last changes fastest.
Arguments:
- tokens: bfloat16 [64, 3072, 1024], P('chan', 'patch'), may hold values from -6 to 6
- table: int32 [64], P('chan'), may hold values from 0 to 1, as said below
- w_key: bfloat16 [1024, 1024], replicated, may hold values from -0.1875 to 0.1875
- w_value: bfloat16 [1024, 1024], replicated, may hold values from -0.1875 to 0.1875
- query_one: float32 [1024], replicated, may hold values from -100 to 100
- w_key_two: bfloat16 [1024, 1024], replicated, may hold values from -0.1875 to 0.1875
- query_two: float32 [1024], replicated, may hold values from -100 to 100
- cotangent: bfloat16 [16, 192, 1024], P('patch', 'chan'), may hold values from -6 to 6
Outputs:
- token_grad: bfloat16 [64, 3072, 1024], P('chan', 'patch')
- grad_w_key: float32 [1024, 1024], P('patch')
- grad_w_value: float32 [1024, 1024], P('patch')
- grad_w_key_two: float32 [1024, 1024], P('patch')
- grad_query_one: float32 [1024], replicated
- grad_query_two: float32 [1024], replicated
Inputs may be any that keep to these rules, and one draw needn't show every extreme that they name: `table`: in every aligned block of 4 channels each of the 2 group numbers appears at least once.
All inputs are finite; a program needn't handle non-finite values.
Results may differ from a plain program's by a relative error of at most 0.0087.
Values may be sent and summed in bfloat16 or wider, within the bound.
No kernel may reach another device: no remote copies, remote signals or barrier semaphores. Data moves between devices by JAX's collectives and lax.ppermute only.
A program may use at most 128 MiB of HBM per device.

v0:
```python
import math

import jax
import jax.numpy as jnp
from jax import lax
from jax.sharding import PartitionSpec as P

D = 1024
HEADS = 16
HD = 64
GPD = 2


def dot_first(left, right):
    return lax.dot_general(
        left, right, (((0,), (0,)), ((), ())), preferred_element_type=jnp.float32
    )


def dot_second(left, right):
    return lax.dot_general(
        left, right, (((1,), (1,)), ((), ())), preferred_element_type=jnp.float32
    )


def level_one(tokens, onehot, w_key, w_value, query_one):
    chans, rows, width = tokens.shape
    scale_one = 1.0 / math.sqrt(HD)
    flat = tokens.reshape(chans * rows, width)
    keys = jnp.dot(flat, w_key, preferred_element_type=jnp.float32).reshape(chans, rows, HEADS, HD)
    values = jnp.dot(flat, w_value, preferred_element_type=jnp.float32).reshape(
        chans, rows, HEADS, HD
    )
    scores = jnp.sum(keys * query_one.reshape(HEADS, HD), -1) * scale_one
    masked = jnp.where(onehot.T[:, :, None, None] > 0, scores[None], -jnp.inf)
    top = jnp.max(masked, 1)
    high = lax.Precision.HIGHEST
    chan_top = jnp.einsum("cg,gbh->cbh", onehot, top, precision=high)
    expo = jnp.exp(scores - chan_top)
    total = jnp.einsum("cg,cbh->gbh", onehot, expo, precision=high)
    weights = expo / jnp.einsum("cg,gbh->cbh", onehot, total, precision=high)
    agg = jnp.einsum("cg,cbhk->gbhk", onehot, weights[..., None] * values, precision=high)
    agg = agg.reshape(onehot.shape[1], rows, width).astype(jnp.bfloat16)
    return (agg, keys, values, weights)


def level_one_back(tokens, onehot, w_key, w_value, query_one, keys, values, weights, agg_grad):
    chans, rows, width = tokens.shape
    scale_one = 1.0 / math.sqrt(HD)
    high = lax.Precision.HIGHEST
    agg_f = agg_grad.astype(jnp.float32).reshape(onehot.shape[1], rows, HEADS, HD)
    chan_grad = jnp.einsum("cg,gbhk->cbhk", onehot, agg_f, precision=high)
    value_grad = (weights[..., None] * chan_grad).reshape(chans * rows, width).astype(jnp.bfloat16)
    dw_one = jnp.sum(chan_grad * values, -1)
    group_inner = jnp.einsum("cg,cbh->gbh", onehot, weights * dw_one, precision=high)
    score_grad = weights * (dw_one - jnp.einsum("cg,gbh->cbh", onehot, group_inner, precision=high))
    key_grad = (
        (score_grad[..., None] * query_one.reshape(HEADS, HD) * scale_one)
        .reshape(chans * rows, width)
        .astype(jnp.bfloat16)
    )
    query_grad = jnp.sum(score_grad[..., None] * keys, (0, 1)).reshape(width) * scale_one
    token_grad = (dot_second(key_grad, w_key) + dot_second(value_grad, w_value)).astype(
        jnp.bfloat16
    )
    return (
        token_grad.reshape(chans, rows, width),
        tokens.reshape(chans * rows, width),
        key_grad,
        value_grad,
        query_grad,
    )


def level_two_scores(agg, w_key_two, query_two):
    groups, rows, width = agg.shape
    keys_two = jnp.dot(
        agg.reshape(groups * rows, width), w_key_two, preferred_element_type=jnp.float32
    )
    keys_two = keys_two.reshape(groups, rows, HEADS, HD)
    scores_two = jnp.sum(keys_two * query_two.reshape(HEADS, HD), -1) * (1.0 / math.sqrt(HD))
    return (keys_two, scores_two)


def cot_products(agg, cot_f):
    groups, rows, width = agg.shape
    return jnp.sum(cot_f[None] * agg.astype(jnp.float32).reshape(groups, rows, HEADS, HD), -1)


def level_two_back(agg, keys_two, weights_two, inner_two, dw_two, cot_f, w_key_two, query_two):
    groups, rows, width = agg.shape
    scale_one = 1.0 / math.sqrt(HD)
    value_part = (weights_two[..., None] * cot_f[None]).reshape(groups * rows, width)
    score_grad = weights_two * (dw_two - inner_two[None])
    key_grad = (
        (score_grad[..., None] * query_two.reshape(HEADS, HD) * scale_one)
        .reshape(groups * rows, width)
        .astype(jnp.bfloat16)
    )
    agg_grad = (
        (value_part + dot_second(key_grad, w_key_two))
        .astype(jnp.bfloat16)
        .reshape(groups, rows, width)
    )
    query_grad = jnp.sum(score_grad[..., None] * keys_two, (0, 1)).reshape(width) * scale_one
    return (agg_grad, key_grad, query_grad)


def shards(tokens, table, w_key, w_value, query_one, w_key_two, query_two, cotangent):
    onehot = (table[:, None] == jnp.arange(GPD, dtype=jnp.int32)[None]).astype(jnp.float32)
    agg, keys, values, weights = level_one(tokens, onehot, w_key, w_value, query_one)
    owned = lax.all_to_all(agg, "chan", split_axis=1, concat_axis=0, tiled=True)
    cot_f = cotangent[0].astype(jnp.float32).reshape(owned.shape[1], HEADS, HD)
    keys_two, scores_two = level_two_scores(owned, w_key_two, query_two)
    expo = jnp.exp(scores_two - jnp.max(scores_two, 0))
    weights_two = expo / jnp.sum(expo, 0)
    dw_two = cot_products(owned, cot_f)
    inner_two = jnp.sum(weights_two * dw_two, 0)
    owned_grad, key_grad_two, qg_two = level_two_back(
        owned, keys_two, weights_two, inner_two, dw_two, cot_f, w_key_two, query_two
    )
    agg_grad = lax.all_to_all(owned_grad, "chan", split_axis=0, concat_axis=1, tiled=True)
    rows_two = owned.reshape(-1, D)
    token_grad, flat, key_grad, value_grad, qg_one = level_one_back(
        tokens, onehot, w_key, w_value, query_one, keys, values, weights, agg_grad
    )
    qg_one, qg_two = lax.psum((qg_one, qg_two), ("chan", "patch"))
    mine = lax.psum_scatter(
        jnp.concatenate(
            [
                dot_first(flat, key_grad),
                dot_first(flat, value_grad),
                dot_first(rows_two, key_grad_two),
            ],
            1,
        ),
        "patch",
        scatter_dimension=0,
        tiled=True,
    )
    mine = lax.psum(mine, "chan")
    return (token_grad, mine[:, :D], mine[:, D : 2 * D], mine[:, 2 * D :], qg_one, qg_two)


def solution(mesh):
    return jax.shard_map(
        shards,
        mesh=mesh,
        in_specs=(
            P("chan", "patch", None),
            P("chan"),
            P(),
            P(),
            P(),
            P(),
            P(),
            P("patch", "chan", None),
        ),
        out_specs=(
            P("chan", "patch", None),
            P("patch", None),
            P("patch", None),
            P("patch", None),
            P(),
            P(),
        ),
        check_vma=False,
    )
```

profile of v0, /device:TPU:8, one launch (start us, length us, event | category | flops | bytes accessed | tf_op | source)
XLA Modules:
  0.0 514.2 jit_solution(14715181382026995020)
XLA Ops:
  8.7 3.9 copy.198
  12.7 4.0 copy.203
  16.6 6.0 %multiply_reduce_fusion.2 = (f32[4,192,16]{1,2,0:T(8,128)S(1)}, f32[4,192,16,64]{1,3,2,0:T(8,128)}) fusion(f32[16,64]{1,0:T(8,128)S(1)} %mul.209, bf16[16,64,1024,1]{2,1,0,3:T(8,128)(2,1)} %bitcast.113, bf16[4,192,1024]{2,1,0:T(8,128)(2,1)S(1)} %copy-done), kind=kOutput, calls=%fused_computation.8 | convolution fusion | flops 1612173312 | bytes 6868992 | tf_op jit(solution)/shard_map/dot_general | solution.py:30
  24.2 4.4 broadcast_multiply_fusion
  28.6 5.5 %fusion.10 = bf16[2,192,16,64]{1,0,3,2:T(2,128)(2,1)S(1)} fusion(f32[4,192,16,64]{1,3,2,0:T(8,128)S(1)} %get-tuple-element.71, s32[4]{0:T(128)S(1)} %copy-done.10), kind=kOutput, calls=%fused_computation.28 | convolution fusion | flops 19267592 | bytes 3932176 | tf_op jit(solution)/shard_map/cg,cbhk->gbhk/dot_general | solution.py:42
  34.1 3.4 copy.205
  37.5 10.8 %all-to-all-start = ((bf16[2,192,1024]{2,0,1:T(2,128)(2,1)}), bf16[2,192,1024]{2,0,1:T(2,128)(2,1)S(1)}, u32[]{:S(2)}, u32[]{:S(2)}) async-start(bf16[2,192,1024]{2,0,1:T(2,128)(2,1)} %copy.205), calls=%async_computation | async-start | bytes 1572864 | tf_op jit(solution)/shard_map/all_to_all | solution.py:112
  48.5 4.0 copy.208
  52.5 20.2 %all-to-all-done = bf16[2,192,1024]{2,0,1:T(2,128)(2,1)S(1)} async-done(((bf16[2,192,1024]{2,0,1:T(2,128)(2,1)}), bf16[2,192,1024]{2,0,1:T(2,128)(2,1)S(1)}, u32[]{:S(2)}, u32[]{:S(2)}) %all-to-all-start) | async-done | bytes 786464 | tf_op jit(solution)/shard_map/all_to_all | solution.py:112
  72.8 1.6 copy_bitcast_fusion.2
  76.4 5.5 %multiply_reduce_fusion.5 = (f32[32,12,16]{0,2,1:T(8,128)S(1)}, f32[32,12,16,64]{3,0,2,1:T(8,128)}) fusion(f32[16,64]{1,0:T(8,128)S(1)} %mul.216, bf16[16,64,1024,1]{2,1,0,3:T(8,128)(2,1)} %bitcast.112, bf16[32,12,1024,1]{2,0,1,3:T(8,128)(2,1)} %reshape.195), kind=kOutput, calls=%fused_computation.14 | convolution fusion | flops 806086656 | bytes 4485120 | tf_op jit(solution)/shard_map/dot_general | solution.py:77
  81.9 1.9 fusion.49
  83.9 2.4 copy.211
  86.3 3.9 reshape.189
  90.2 2.8 multiply_reduce_fusion.4
  94.6 2.2 copy.210
  96.8 3.7 mul.224
  100.5 2.2 mul.228.clone
  102.7 3.7 mul.229
  106.4 3.5 add_convert_fusion.1
  111.1 4.3 all-to-all-start.1
  116.9 2.4 multiply_reduce_fusion.3
  120.0 1.9 convert_element_type.89
  121.9 4.6 fusion.50
  126.5 17.3 %all-to-all-done.1 = bf16[32,12,1024]{2,1,0:T(8,128)(2,1)} async-done(((bf16[32,12,1024]{2,1,0:T(8,128)(2,1)}), bf16[32,12,1024]{2,1,0:T(8,128)(2,1)}, u32[]{:S(2)}, u32[]{:S(2)}) %all-to-all-start.1) | async-done | bytes 786464 | tf_op jit(solution)/shard_map/all_to_all | solution.py:122
  143.8 2.9 copy.260
  146.7 2.9 reshape.184
  149.7 3.1 copy.216
  152.8 2.9 fusion.27
  155.7 1.9 multiply_convert_fusion.1
  157.7 3.1 copy.223
  160.7 4.1 convert_element_type.84
  165.4 3.1 multiply_reduce_fusion
  168.4 3.1 copy.224
  171.5 4.7 convert_element_type.87
  176.2 3.2 convolution_bitcast_fusion.1
  179.4 1.8 convolution_bitcast_fusion
  181.6 5.6 %pad_maximum_fusion = f32[1024,3072]{0,1:T(8,128)} fusion(f32[1024,1024]{0,1:T(8,128)S(1)} %copy-done.1, f32[1024,1024]{0,1:T(8,128)S(1)} %convolution_bitcast_fusion, f32[1024,1024]{0,1:T(8,128)S(1)} %convolution_bitcast_fusion.1), kind=kLoop, calls=%fused_computation.1 | loop fusion | flops 6291456 | bytes 25165824 | tf_op jit(solution)/shard_map/concatenate | solution.py:129
  187.2 12.6 %copy.234 = f32[1024,3072]{1,0:T(8,128)} copy(f32[1024,3072]{0,1:T(8,128)} %pad_maximum_fusion) | data formatting | bytes 25165824
  199.9 2.5 mul.237.clone
  202.4 5.6 %mul.238 = f32[768,1024]{0,1:T(8,128)} reshape(f32[4,192,16,64]{1,0,3,2:T(4,128)} %mul.237.clone) | data formatting | bytes 6291456 | tf_op jit(solution)/shard_map/mul | solution.py:58
  208.0 6.3 %fusion.3 = f32[768,1024]{1,0:T(8,128)} fusion(bf16[1024,1024]{1,0:T(8,128)(2,1)} %param.10, f32[768,1024]{0,1:T(8,128)} %mul.238, f32[1024]{0:T(1024)S(1)} %copy-done.12), kind=kOutput, calls=%fused_computation.18 | convolution fusion | flops 1612972032 | bytes 8392704 | tf_op jit(solution)/shard_map/dot_general | solution.py:21
  214.3 122.5 %reduce-scatter.4.cloned.1.call-done = f32[64,3072]{1,0:T(8,128)} async-done(((f32[1024,3072]{1,0:T(8,128)}), f32[64,3072]{1,0:T(8,128)}) %reduce-scatter.4.cloned.1.call-update) | async-done | bytes 786448
  336.7 2.8 copy.235
  339.6 78.4 %all-reduce = (f32[1024]{0:T(1024)}, f32[1024]{0:T(1024)}) all-reduce(f32[1024]{0:T(1024)S(1)} %mul.252, f32[1024]{0:T(1024)S(1)} %mul.255), channel_id=1, replica_groups=mesh['chan'=16,'patch'=16] {'chan','patch'}, use_global_device_ids=true, to_apply=%region_11.12 | all-reduce | flops 2048 | bytes 16384 | tf_op jit(solution)/shard_map/psum | solution.py:127
  418.0 5.5 %add_convert_fusion = bf16[768,1024]{1,0:T(8,128)(2,1)} fusion(f32[768,1024]{1,0:T(8,128)} %fusion.3, bf16[768,1024]{0,1:T(8,128)(2,1)S(1)} %convert_element_type.84, bf16[1024,1024]{1,0:T(8,128)(2,1)} %param.11), kind=kOutput, calls=%fused_computation.11 | convolution fusion | flops 1612185600 | bytes 8388608 | tf_op jit(solution)/shard_map/dot_general | solution.py:21
  423.6 79.4 %all-reduce.3.cloned.1.call-done = f32[64,3072]{0,1:T(8,128)} async-done(((f32[64,3072]{0,1:T(8,128)}), f32[64,3072]{0,1:T(8,128)}) %all-reduce.3.cloned.1.call-update) | async-done | bytes 786448 | tf_op jit(solution)/shard_map/psum | solution.py:141
  503.0 1.5 fusion.48
  (63 shorter events, 13.8 us)
Async XLA Ops:
  7.2 9.5 %copy-start = (bf16[4,192,1024]{2,1,0:T(8,128)(2,1)S(1)}, bf16[4,192,1024]{2,1,0:T(8,128)(2,1)}, u32[]{:S(2)}) copy-start(bf16[4,192,1024]{2,1,0:T(8,128)(2,1)} %param.8) | copy-start | bytes 4718596
  16.6 6.2 %copy-start.10 = (s32[4]{0:T(128)S(1)}, s32[4]{0:T(128)}, u32[]{:S(2)}) copy-start(s32[4]{0:T(128)} %param.9) | copy-start | bytes 52
  16.6 7.6 %copy-start.4 = (bf16[1024,1024]{0,1:T(8,128)(2,1)S(1)}, bf16[1024,1024]{0,1:T(8,128)(2,1)}, u32[]{:S(2)}) copy-start(bf16[1024,1024]{0,1:T(8,128)(2,1)} %copy.203) | copy-start | bytes 6291460
  23.6 0.6 copy-start.5
  24.2 4.4 copy-start.7
  34.1 14.3 %copy-start.11 = (f32[1024]{0:T(1024)S(1)}, f32[1024]{0:T(1024)}, u32[]{:S(2)}) copy-start(f32[1024]{0:T(1024)} %param.14) | copy-start | bytes 12292
  34.1 14.3 %copy-start.9 = (bf16[1,12,1024]{2,1,0:T(8,128)(2,1)S(1)}, bf16[1,12,1024]{2,1,0:T(8,128)(2,1)}, u32[]{:S(2)}) copy-start(bf16[1,12,1024]{2,1,0:T(8,128)(2,1)} %param.15) | copy-start | bytes 73732
  37.5 35.2 %all-to-all-start = ((bf16[2,192,1024]{2,0,1:T(2,128)(2,1)}), bf16[2,192,1024]{2,0,1:T(2,128)(2,1)S(1)}, u32[]{:S(2)}, u32[]{:S(2)}) async-start(bf16[2,192,1024]{2,0,1:T(2,128)(2,1)} %copy.205), calls=%async_computation | async-start | bytes 1572864 | tf_op jit(solution)/shard_map/all_to_all | solution.py:112
  76.4 7.5 %copy-start.2 = (f32[16,2,12,1024]{3,0,2,1:T(8,128)S(1)}, f32[16,2,12,1024]{3,0,2,1:T(8,128)}, u32[]{:S(2)}) copy-start(f32[16,2,12,1024]{3,0,2,1:T(8,128)} %get-tuple-element.64) | copy-start | bytes 4718596
  111.1 32.8 %all-to-all-start.1 = ((bf16[32,12,1024]{2,1,0:T(8,128)(2,1)}), bf16[32,12,1024]{2,1,0:T(8,128)(2,1)}, u32[]{:S(2)}, u32[]{:S(2)}) async-start(bf16[32,12,1024]{2,1,0:T(8,128)(2,1)} %reshape.183), calls=%async_computation.1 | async-start | bytes 2097152 | tf_op jit(solution)/shard_map/all_to_all | solution.py:122
  115.4 221.3 %reduce-scatter.4.cloned.1.call-start = ((), (), s32[]{:S(2)}) async-start(), calls=%async_computation.4 | async-start | bytes 13369344
  152.8 3.0 copy-start.3
  152.8 3.0 copy-start.8
  160.7 4.1 copy-start.6
  179.4 2.2 copy-start.1
  199.8 303.2 %all-reduce.3.cloned.1.call-start = ((), (), s32[]{:S(2)}) async-start(), calls=%async_computation.3 | async-start | bytes 3145728 | tf_op jit(solution)/shard_map/psum | solution.py:141
  202.4 5.6 %copy-start.12 = (f32[1024]{0:T(1024)S(1)}, f32[1024]{0:T(1024)}, u32[]{:S(2)}) copy-start(f32[1024]{0:T(1024)} %param.12) | copy-start | bytes 12292
Sparse Core Ops, SparseCore 0:
  199.9 136.8 reduce-scatter.3
  339.7 163.2 all-reduce.2
where the time goes:
time: 523 us; the launch traced here: 514 us
  waiting for transfers between devices  239 us (46%)
  local copies, waits for them, and re-layouts  94.3 us (18%)
  blocking collectives  78.4 us (15%)
  matrix products  50.6 us (10%)
  other arithmetic  21.4 us (4%)
  starting transfers between devices  15.4 us (3%)
  between operations  14.7 us (3%)
    unnamed x3, waiting for transfers between devices  122 us
    psum x1, waiting for transfers between devices, shards(): mine = lax.psum(mine, 'chan')  79.4 us
    psum x1, blocking collectives, shards(): qg_one, qg_two = lax.psum((qg_one, qg_two), ('chan', 'patch'))  78.4 us
    unnamed x35, local copies, waits for them, and re-layouts  31.1 us
    all_to_all x1, waiting for transfers between devices, shards(): owned = lax.all_to_all(agg, 'chan', split_axis=1, concat_axis=0, tiled=True)  20.2 us
    all_to_all x1, waiting for transfers between devices, shards(): lax.all_to_all(owned_grad, 'chan', split_axis=0, concat_axis=1, tiled=True)  17.3 us
    dot_general x3, matrix products, dot_second(): lax.dot_general(left, right, (((1,), (1,)), ((), ())), preferred_element_...  15.4 us
    all_to_all x1, starting transfers between devices, shards(): owned = lax.all_to_all(agg, 'chan', split_axis=1, concat_axis=0, tiled=True)  10.8 us
  transfers between devices with their start and end apart: 4, of which 4 were waited for; matrix products, arithmetic and copies ran while one was open for 7% of the time, Pallas kernels for 0%

commit v1 on v0

v1 whole, which is shorter than its diff:
```python
import functools

import jax
import jax.numpy as jnp
from jax import lax
from jax.experimental import pallas as pl
from jax.experimental.pallas import tpu as pltpu
from jax.sharding import PartitionSpec as P

D = 1024
HEADS = 16
HD = 64
SHIFT = 6
SCALE = 0.125
CH = 4
GR = 2
ROWS = 192
BLK = 64
NB = ROWS // BLK
TOK = CH * BLK
AGG = GR * BLK
SLAB = 72
F32 = jnp.float32
BF16 = jnp.bfloat16
LIMIT = 40 * 2**20


def nn(a, b):
    return lax.dot_general(a, b, (((1,), (0,)), ((), ())), preferred_element_type=F32)


def nt(a, b):
    return lax.dot_general(a, b, (((1,), (1,)), ((), ())), preferred_element_type=F32)


def split2(x):
    high = x.astype(BF16)
    return high, (x - high.astype(F32)).astype(BF16)


def split3(x):
    high = x.astype(BF16)
    rest = x - high.astype(F32)
    middle = rest.astype(BF16)
    return high, middle, (rest - middle.astype(F32)).astype(BF16)


def spread(copies):
    row = lax.broadcasted_iota(jnp.int32, (copies * HEADS, D), 0) & (HEADS - 1)
    col = lax.broadcasted_iota(jnp.int32, (copies * HEADS, D), 1) >> SHIFT
    return jnp.where(row == col, 1.0, 0.0).astype(BF16)


def expand(x, heads2):
    return nn(jnp.concatenate(split2(x), 1), heads2)


def head_sum(x, heads):
    high, low = split2(x)
    return nt(high, heads) + nt(low, heads)


def fold(weight, query):
    parts = [p.astype(F32) for p in split3(query * SCALE)]
    row = lax.broadcasted_iota(jnp.int32, (HEADS, D), 0)
    col = lax.broadcasted_iota(jnp.int32, (HEADS, D), 1) >> SHIFT
    wide = [jnp.where(row == col, p, 0.0).astype(BF16) for p in parts]
    out = nt(weight, jnp.concatenate(wide, 0))
    total = out[:, :HEADS] + out[:, HEADS : 2 * HEADS] + out[:, 2 * HEADS :]
    return jnp.concatenate(split3(total), 1)


def folded_dot(x, folded):
    out = nn(x, folded)
    return out[:, :HEADS] + out[:, HEADS : 2 * HEADS] + out[:, 2 * HEADS :]


def folded_back(x, folded):
    high, low = split2(x)
    right = jnp.concatenate(
        [folded[:, :HEADS], folded[:, HEADS : 2 * HEADS], folded[:, :HEADS]], 1
    )
    return nt(jnp.concatenate([high, high, low], 1), right)


def forward_kernel(
    table, tok, w_value, w_key, w_key_two, query_one, query_two,
    values, weights, agg, agg_t, tok_t, scores_two, fold_one, fold_two,
):
    @pl.when(pl.program_id(0) == 0)
    def _():
        fold_one[...] = fold(w_key[...], query_one[...])
        fold_two[...] = fold(w_key_two[...], query_two[...])

    flat = tok[...].reshape(TOK, D)
    tok_t[...] = flat.T
    scores = folded_dot(flat, fold_one[...])
    vals = nn(flat, w_value[...])
    values[...] = vals
    group = [table[c] for c in range(CH)]
    score = [scores[c * BLK : (c + 1) * BLK] for c in range(CH)]
    top = [
        functools.reduce(
            jnp.maximum, [jnp.where(group[c] == g, score[c], -jnp.inf) for c in range(CH)]
        )
        for g in range(GR)
    ]
    expo = [jnp.exp(score[c] - jnp.where(group[c] == 0, top[0], top[1])) for c in range(CH)]
    total = [sum(jnp.where(group[c] == g, expo[c], 0.0) for c in range(CH)) for g in range(GR)]
    weight = jnp.concatenate(
        [expo[c] / jnp.where(group[c] == 0, total[0], total[1]) for c in range(CH)], 0
    )
    weights[...] = weight
    mixed = expand(weight, spread(2)) * vals
    part = [mixed[c * BLK : (c + 1) * BLK] for c in range(CH)]
    both = jnp.concatenate(
        [sum(jnp.where(group[c] == g, part[c], 0.0) for c in range(CH)) for g in range(GR)], 0
    ).astype(BF16)
    agg[...] = both
    agg_t[...] = both.T
    scores_two[...] = folded_dot(both, fold_two[...])


def pack(x):
    return jnp.concatenate([x[24 * k : 24 * k + 24] for k in range(8)], 1)


def unpack(x):
    return jnp.concatenate([x[:, HEADS * k : HEADS * (k + 1)] for k in range(8)], 0)


def stats_kernel(agg, cot, scores_two, dw_two, stats):
    heads = spread(1)
    score, grad = [[], []], [[], []]
    for b in range(NB):
        cot_f = cot[b * BLK : (b + 1) * BLK].astype(F32)
        for g in range(GR):
            rows = slice(b * AGG + g * BLK, b * AGG + (g + 1) * BLK)
            dw = head_sum(agg[rows].astype(F32) * cot_f, heads)
            dw_two[rows] = dw
            grad[g].append(dw)
            score[g].append(scores_two[rows])
    score = [jnp.concatenate(s, 0) for s in score]
    grad = [jnp.concatenate(s, 0) for s in grad]
    top = jnp.maximum(score[0], score[1])
    expo = [jnp.exp(s - top) for s in score]
    total = expo[0] + expo[1]
    log_total = top + jnp.log(total)
    inner = (expo[0] * grad[0] + expo[1] * grad[1]) / total
    both = jnp.concatenate([pack(log_total), pack(inner)], 0)
    for k in range(16):
        stats[k] = both


def backward_kernel(
    table, core, stats, agg_t, tok_t, cot, scores_two, dw_two, values, weights,
    w_key, w_key_two, fold_two,
    value_grad, score_grad, send, keep, sums,
):
    heads, heads2 = spread(1), spread(2)
    group = [table[c] for c in range(CH)]
    logs = stats[:, :24, :]
    top = jnp.max(logs, 0)
    expo = jnp.exp(logs - top[None])
    total = jnp.sum(expo, 0)
    inner = unpack(jnp.sum(expo * stats[:, 24:, :], 0) / total)
    log_total = unpack(top + jnp.log(total))
    grads_two = []
    for b in range(NB):
        rows = slice(b * BLK, (b + 1) * BLK)
        arows = slice(b * AGG, (b + 1) * AGG)
        trows = slice(b * TOK, (b + 1) * TOK)
        twice = lambda x: jnp.concatenate([x, x], 0)
        w_two = jnp.exp(scores_two[arows] - twice(log_total[rows]))
        s_two = w_two * (dw_two[arows] - twice(inner[rows]))
        grads_two.append(s_two)
        cot_f = cot[rows].astype(F32)
        agg_grad = expand(w_two, heads2) * twice(cot_f) + folded_back(s_two, fold_two[...])
        agg_grad = agg_grad.astype(BF16).astype(F32)
        first, second = agg_grad[:BLK], agg_grad[BLK:]
        chan = jnp.concatenate([jnp.where(group[c] == 0, first, second) for c in range(CH)], 0)
        weight = weights[trows]
        value_grad[trows] = (expand(weight, heads2) * chan).astype(BF16)
        dw = head_sum(chan * values[trows], heads)
        wdw = weight * dw
        part = [wdw[c * BLK : (c + 1) * BLK] for c in range(CH)]
        inner_one = [
            sum(jnp.where(group[c] == g, part[c], 0.0) for c in range(CH)) for g in range(GR)
        ]
        own = jnp.concatenate(
            [jnp.where(group[c] == 0, inner_one[0], inner_one[1]) for c in range(CH)], 0
        )
        score_grad[trows] = weight * (dw - own)
    for n in range(4):
        cols = slice(n * 256, (n + 1) * 256)
        out = nn(tok_t[...], value_grad[:, cols])
        for p in range(16):
            sums[p * SLAB : p * SLAB + 64, cols] = out[p * 64 : (p + 1) * 64]

    def outer(left, right):
        both = nn(left, jnp.concatenate(split2(right), 1))
        return both[:, :HEADS] + both[:, HEADS:]

    ones = outer(tok_t[...], score_grad[...])
    twos = outer(agg_t[...], jnp.concatenate(grads_two, 0))
    grads = jnp.concatenate([ones, twos, jnp.zeros((D, 128 - 2 * HEADS), F32)], 1).T
    lines = []
    for k, weight in enumerate((w_key, w_key_two)):
        high, low = split2(grads[k * HEADS : (k + 1) * HEADS])
        out = nn(jnp.concatenate([high, low], 0), weight[...])
        out = (out[:HEADS] + out[HEADS:]) * heads.astype(F32)
        lines.append(jnp.sum(out, 0, keepdims=True) * SCALE)
    quads = jnp.concatenate(
        [lines[0][:, :512], lines[0][:, 512:], lines[1][:, :512], lines[1][:, 512:]], 0
    )
    high = quads.astype(BF16).astype(F32)
    small = jnp.concatenate([high, quads - high], 0)
    turned = jnp.concatenate([grads[: 2 * HEADS, 64:], grads[: 2 * HEADS, :64]], 1)
    for p in range(16):
        source = turned if p % 2 else grads
        rows = slice(p * SLAB + 64, (p + 1) * SLAB)
        lanes = slice((p // 2) * 128, (p // 2 + 1) * 128)
        for k in range(4):
            sums[rows, k * 128 : (k + 1) * 128] = source[8 * k : 8 * k + 8, lanes]
        sums[rows, 512:] = small
    mine = core[0]
    for k in range(8):
        away = pl.multiple_of((2 * k + 1 - mine) * SLAB, 8)
        here = pl.multiple_of((2 * k + mine) * SLAB, 8)
        send[k] = sums[pl.ds(away, SLAB), :].astype(BF16)
        keep[k] = sums[pl.ds(here, SLAB), :]


def token_kernel(value_grad, score_grad, w_value, fold_one, out):
    grad = nt(value_grad[...], w_value[...]) + folded_back(score_grad[...], fold_one[...])
    out[...] = grad.astype(BF16).reshape(CH, BLK, D)


def rows_kernel(got, out):
    total = got[0].astype(F32)
    for k in range(1, 8):
        total = total + got[k].astype(F32)
    extra = total[64:]
    tall = [extra[:, k * 128 : k * 128 + 64] for k in range(4)]
    line = extra[:4, 512:] + extra[4:, 512:]
    extra = jnp.concatenate([t[:4] for t in tall] + [t[4:] for t in tall] + [line], 1)
    for c in range(16):
        out[c] = jnp.concatenate([total[4 * c : 4 * c + 4], extra], 0).astype(BF16)


def chans_kernel(got, rows, extra):
    total = got[0].astype(F32)
    for k in range(1, 16):
        total = total + got[k].astype(F32)
    for c in range(16):
        rows[c] = total[:4]
    extra[...] = total[4:]


def small_kernel(extra, query_one, query_two, grad_key, grad_key_two, line_one, line_two):
    x = extra[...]
    tall = [x[:, k * 64 : (k + 1) * 64] for k in range(8)]
    grads = jnp.concatenate(
        [jnp.concatenate([tall[k], tall[k + 4]], 0) for k in range(4)], 0
    )
    grads = jnp.concatenate([grads, jnp.zeros((32, 64), F32)], 0)
    turned = jnp.concatenate([grads, jnp.zeros((64, 64), F32)], 1).T[:64]
    heads3 = spread(3)
    for k, (query, out) in enumerate(((query_one, grad_key), (query_two, grad_key_two))):
        part = turned[:, k * HEADS : (k + 1) * HEADS]
        out[...] = nn(jnp.concatenate(split3(part), 1), heads3) * (query[...] * SCALE)
    line_one[:, :512] = x[0:1, 512:]
    line_one[:, 512:] = x[1:2, 512:]
    line_two[:, :512] = x[2:3, 512:]
    line_two[:, 512:] = x[3:4, 512:]


def shape(dims, dtype):
    return jax.ShapeDtypeStruct(dims, dtype)


SMEM = pl.BlockSpec(memory_space=pltpu.SMEM)


def whole(dims):
    return pl.BlockSpec(dims, lambda i: (0,) * len(dims))


def call(kernel, out_shape, flops, nbytes, **kw):
    return pl.pallas_call(
        kernel,
        out_shape=out_shape,
        compiler_params=pltpu.CompilerParams(vmem_limit_bytes=LIMIT),
        cost_estimate=pl.CostEstimate(flops=flops, bytes_accessed=nbytes, transcendentals=0),
        **kw,
    )


def shards(tokens, table, w_key, w_value, query_one, w_key_two, query_two, cotangent):
    query_one, query_two = query_one.reshape(1, D), query_two.reshape(1, D)
    tiled = jnp.broadcast_to(cotangent, (16, ROWS // 16, D)).reshape(ROWS, D)
    cot = lax.all_to_all(tiled, "chan", 0, 0, tiled=True)
    full = whole((D, D))
    by_rows = lambda n, w: pl.BlockSpec((n, w), lambda i: (i, 0))
    by_cols = lambda n: pl.BlockSpec((D, n), lambda i: (0, i))
    token_spec = pl.BlockSpec((CH, BLK, D), lambda i: (0, i, 0))
    values, weights, agg, agg_t, tok_t, scores_two, fold_one, fold_two = call(
        forward_kernel,
        (
            shape((NB * TOK, D), F32),
            shape((NB * TOK, HEADS), F32),
            shape((NB * AGG, D), BF16),
            shape((D, NB * AGG), BF16),
            shape((D, NB * TOK), BF16),
            shape((NB * AGG, HEADS), F32),
            shape((D, 3 * HEADS), BF16),
            shape((D, 3 * HEADS), BF16),
        ),
        4 * 10**9,
        16 * 10**6,
        grid=(NB,),
        in_specs=[SMEM, token_spec, full, full, full, whole((1, D)), whole((1, D))],
        out_specs=(
            by_rows(TOK, D),
            by_rows(TOK, HEADS),
            by_rows(AGG, D),
            by_cols(AGG),
            by_cols(TOK),
            by_rows(AGG, HEADS),
            whole((D, 3 * HEADS)),
            whole((D, 3 * HEADS)),
        ),
    )(table, tokens, w_value, w_key, w_key_two, query_one, query_two)
    dw_two, stats = call(
        stats_kernel,
        (shape((NB * AGG, HEADS), F32), shape((16, 48, 128), F32)),
        10**9,
        2 * 10**6,
    )(agg, cot, scores_two)
    stats = lax.all_to_all(stats, "chan", 0, 0, tiled=True)
    core = lax.rem(lax.axis_index("patch"), 2).astype(jnp.int32).reshape(1)
    vmem = pl.BlockSpec(memory_space=pltpu.VMEM)
    value_grad, score_grad, send, keep = call(
        backward_kernel,
        (
            shape((NB * TOK, D), BF16),
            shape((NB * TOK, HEADS), F32),
            shape((8, SLAB, D), BF16),
            shape((8, SLAB, D), F32),
        ),
        4 * 10**9,
        16 * 10**6,
        in_specs=[SMEM, SMEM] + [vmem] * 11,
        scratch_shapes=[pltpu.VMEM((16 * SLAB, D), F32)],
    )(
        table, core, stats, agg_t, tok_t, cot, scores_two, dw_two, values, weights,
        w_key, w_key_two, fold_two,
    )
    got = lax.ppermute(send, "patch", [(i, i ^ 1) for i in range(16)])
    pairs = (keep + got.astype(F32)).astype(BF16)
    same_core = [[i for i in range(16) if i % 2 == k] for k in range(2)]
    got = lax.all_to_all(pairs, "patch", 0, 0, tiled=True, axis_index_groups=same_core)
    token_grad = call(
        token_kernel,
        shape((CH, ROWS, D), BF16),
        2 * 10**9,
        6 * 10**6,
        grid=(NB,),
        in_specs=[by_rows(TOK, D), by_rows(TOK, HEADS), full, whole((D, 3 * HEADS))],
        out_specs=token_spec,
    )(value_grad, score_grad, w_value, fold_one)
    rows = call(rows_kernel, shape((16, 8, D), BF16), 10**6, 2 * 10**6)(got)
    rows = lax.all_to_all(rows, "chan", 0, 0, tiled=True)
    rows, extra = call(
        chans_kernel, (shape((16, 4, D), F32), shape((4, D), F32)), 10**6, 10**6
    )(rows)
    rows = lax.all_to_all(rows, "chan", 0, 0, tiled=True)
    grad_key, grad_key_two, line_one, line_two = call(
        small_kernel,
        (shape((64, D), F32), shape((64, D), F32), shape((1, D), F32), shape((1, D), F32)),
        10**8,
        10**6,
    )(extra, query_one, query_two)
    return (
        token_grad,
        grad_key,
        rows.reshape(64, D),
        grad_key_two,
        line_one.reshape(D),
        line_two.reshape(D),
    )


def solution(mesh):
    return jax.shard_map(
        shards,
        mesh=mesh,
        in_specs=(
            P("chan", "patch", None),
            P("chan"),
            P(),
            P(),
            P(),
            P(),
            P(),
            P("patch", "chan", None),
        ),
        out_specs=(
            P("chan", "patch", None),
            P("patch", None),
            P("patch", None),
            P("patch", None),
            P(),
            P(),
        ),
        check_vma=False,
    )
```

time: 523 us -> 134 us (0.26); the launches traced: 514 us -> 133 us
  waiting for transfers between devices: 239 us -> 27.1 us
  local copies, waits for them, and re-layouts: 94.3 us -> 23.1 us
  matrix products: 50.6 us -> 0 us
  blocking collectives: 78.4 us -> 37.6 us
  Pallas kernels: 0 us -> 22.5 us
  other arithmetic: 21.4 us -> 0.43 us
  between operations: 14.7 us -> 0.84 us
  starting transfers between devices: 15.4 us -> 21.4 us
    unnamed x3 -> x0, waiting for transfers between devices: 122 us -> none
    psum x1 -> x0, waiting for transfers between devices: 79.4 us -> none  [shards(): mine = lax.psum(mine, 'chan')]
    psum x1 -> x0, blocking collectives: 78.4 us -> none  [shards(): qg_one, qg_two = lax.psum((qg_one, qg_two), ('chan', 'patch'))]
    dot_general x16 -> x0, matrix products: 50.6 us -> none  [the longest x3 15.4 us: dot_second(): lax.dot_general(left, right, (((1,), (1,)), ((), ())), preferred_element_...]
    all_to_all x0 -> x2, blocking collectives: none -> 37.6 us  [the longest x1 21.8 us: shards(): lax.all_to_all(pairs, 'patch', 0, 0, tiled=True, axis_index_groups=same_c...]
    convert_element_type x10 -> x0, local copies, waits for them, and re-layouts: 27.3 us -> none  [the longest x2 7.79 us: level_one_back(): key_grad = (score_grad[..., None] * query_one.reshape(HEADS, HD) * scale_...]
    pallas_call x0 -> x7, Pallas kernels: none -> 22.5 us  [the longest x1 7.87 us: shards(): call(backward_kernel, (shape((NB * TOK, D), BF16), shape((NB * TOK, HEADS...]
    mul x12 -> x0, local copies, waits for them, and re-layouts: 20.9 us -> none  [the longest x2 8.06 us: level_one_back(): score_grad[..., None] * query_one.reshape(HEADS, HD) * scale_one]
  transfers between devices with their start and end apart: 4 -> 4, of which waited for: 4 -> 4; matrix products, arithmetic and copies ran while one was open for 7% -> 0% of each run, Pallas kernels for 0% -> 9%
where the time goes in v1:
time: 134 us; the launch traced here: 133 us
  blocking collectives  37.6 us (28%)
  waiting for transfers between devices  27.1 us (20%)
  local copies, waits for them, and re-layouts  23.1 us (17%)
  Pallas kernels  22.5 us (17%)
  starting transfers between devices  21.4 us (16%)
    all_to_all x1, blocking collectives, shards(): lax.all_to_all(pairs, 'patch', 0, 0, tiled=True, axis_index_groups=same_c...  21.8 us
    unnamed x54, local copies, waits for them, and re-layouts  20.5 us
    all_to_all x1, blocking collectives, shards(): rows = lax.all_to_all(rows, 'chan', 0, 0, tiled=True)  15.8 us
    all_to_all x1, waiting for transfers between devices, shards(): stats = lax.all_to_all(stats, 'chan', 0, 0, tiled=True)  15.5 us
    all_to_all x1, starting transfers between devices, shards(): cot = lax.all_to_all(tiled, 'chan', 0, 0, tiled=True)  10.3 us
    pallas_call x1, Pallas kernels, shards(): call(backward_kernel, (shape((NB * TOK, D), BF16), shape((NB * TOK, HEADS...  7.87 us
    pallas_call x1, Pallas kernels, shards(): call(forward_kernel, (shape((NB * TOK, D), F32), shape((NB * TOK, HEADS),...  7.48 us
    all_to_all x1, starting transfers between devices, shards(): stats = lax.all_to_all(stats, 'chan', 0, 0, tiled=True)  7.45 us
  transfers between devices with their start and end apart: 4, of which 4 were waited for; matrix products, arithmetic and copies ran while one was open for 0% of the time, Pallas kernels for 9%

profile of v1, /device:TPU:8, one launch (start us, length us, event | category | flops | bytes accessed | tf_op | source)
XLA Modules:
  0.0 132.9 jit_solution(6146405207896679542)
XLA Ops:
  0.6 0.0 copy-start.9
  0.6 0.0 copy-start.8
  0.7 0.0 copy-start.7
  0.7 0.0 copy-start.6
  0.7 1.7 %broadcast_in_dim.8 = bf16[16,12,1024]{2,1,0:T(8,128)(2,1)} broadcast(bf16[12,1024]{1,0:T(8,128)(2,1)} %bitcast.10), dimensions={1,2} | broadcast | bytes 417792 | tf_op jit(solution)/shard_map/broadcast_in_dim | solution.py:301
  2.4 10.3 %all-to-all-start = ((bf16[16,12,1024]{2,1,0:T(8,128)(2,1)}), bf16[16,12,1024]{2,1,0:T(8,128)(2,1)S(1)}, u32[]{:S(2)}, u32[]{:S(2)}) async-start(bf16[16,12,1024]{2,1,0:T(8,128)(2,1)} %broadcast_in_dim.8), calls=%async_computation | async-start | bytes 1048576 | tf_op jit(solution)/shard_map/all_to_all | solution.py:302
  12.8 0.0 copy-start
  12.8 1.6 %copy-done = bf16[1024,1024]{1,0:T(8,128)(2,1)S(1)} copy-done((bf16[1024,1024]{1,0:T(8,128)(2,1)S(1)}, bf16[1024,1024]{1,0:T(8,128)(2,1)}, u32[]{:S(2)}) %copy-start) | copy-done | bytes 2097176
  14.4 1.6 %copy-done.2 = bf16[1024,1024]{1,0:T(8,128)(2,1)S(1)} copy-done((bf16[1024,1024]{1,0:T(8,128)(2,1)S(1)}, bf16[1024,1024]{1,0:T(8,128)(2,1)}, u32[]{:S(2)}) %copy-start.2) | copy-done | bytes 2097176
  16.0 1.6 %copy-done.4 = bf16[1024,1024]{1,0:T(8,128)(2,1)S(1)} copy-done((bf16[1024,1024]{1,0:T(8,128)(2,1)S(1)}, bf16[1024,1024]{1,0:T(8,128)(2,1)}, u32[]{:S(2)}) %copy-start.4) | copy-done | bytes 2097176
  17.5 7.5 %shard_map.127 = (f32[768,1024]{1,0:T(8,128)}, f32[768,16]{1,0:T(8,128)S(1)}, bf16[384,1024]{1,0:T(8,128)(2,1)S(1)}, bf16[1024,384]{1,0:T(8,128)(2,1)S(1)}, bf16...) custom-call(s32[4]{0:T(128)S(1)} %copy-done.9, ...), custom_call_target="tpu_custom_call" | custom-call | flops 4000000000 | bytes 16000000 | tf_op jit(solution)/shard_map/pallas_call | solution.py:307
  25.0 1.1 copy-done.12
  26.2 0.9 copy-done.14
  27.1 0.9 copy-done.16
  27.9 0.7 copy-done.20
  28.6 2.8 %all-to-all-done = bf16[16,12,1024]{2,1,0:T(8,128)(2,1)S(1)} async-done(((bf16[16,12,1024]{2,1,0:T(8,128)(2,1)}), bf16[16,12,1024]{2,1,0:T(8,128)(2,1)S(1)}, u32[]{:S(2)}, u32[]{:S(2)}) %all-to-all-start) | async-done | bytes 393248 | tf_op jit(solution)/shard_map/all_to_all | solution.py:302
  31.4 0.1 all_to_all.18.cot
  31.5 0.0 copy-done.25
  31.5 0.0 copy-start.15
  31.5 1.1 copy-done.15
  32.6 0.9 copy-done.21
  33.6 1.4 %shard_map.128 = (f32[384,16]{1,0:T(8,128)S(1)}, f32[16,48,128]{2,1,0:T(8,128)}) custom-call(bf16[384,1024]{1,0:T(8,128)(2,1)S(1)} %copy-done.15, bf16[192,1024]{1,0:T(8,128)(2,1)S(1)} %all_to_all.18.cot, f32[384,16]{1,0:T(8,128)S(1)} %copy-done.21), custom_call_target="tpu_custom_call" | custom-call | flops 1000000000 | bytes 2000000 | tf_op jit(solution)/shard_map/pallas_call | solution.py:334
  35.0 0.7 copy-done.23
  35.6 7.4 %all-to-all-start.1 = ((f32[16,48,128]{2,1,0:T(8,128)}), f32[16,48,128]{2,1,0:T(8,128)S(1)}, u32[]{:S(2)}, u32[]{:S(2)}) async-start(f32[16,48,128]{2,1,0:T(8,128)} %get-tuple-element.28), calls=%async_computation.1 | async-start | bytes 786432 | tf_op jit(solution)/shard_map/all_to_all | solution.py:340
  43.1 15.5 %all-to-all-done.1.stats = f32[16,48,128]{2,1,0:T(8,128)S(1)} async-done(((f32[16,48,128]{2,1,0:T(8,128)}), f32[16,48,128]{2,1,0:T(8,128)S(1)}, u32[]{:S(2)}, u32[]{:S(2)}) %all-to-all-start.1) | async-done | bytes 393248 | tf_op jit(solution)/shard_map/all_to_all | solution.py:340
  58.6 1.6 %copy-done.3 = bf16[1024,1024]{1,0:T(8,128)(2,1)S(1)} copy-done((bf16[1024,1024]{1,0:T(8,128)(2,1)S(1)}, bf16[1024,1024]{1,0:T(8,128)(2,1)}, u32[]{:S(2)}) %copy-start.3) | copy-done | bytes 2097176
  60.2 1.4 %copy-done.13 = bf16[1024,768]{1,0:T(8,128)(2,1)S(1)} copy-done((bf16[1024,768]{1,0:T(8,128)(2,1)S(1)}, bf16[1024,768]{1,0:T(8,128)(2,1)}, u32[]{:S(2)}) %copy-start.13) | copy-done | bytes 1572888
  61.6 1.1 copy-done.17
  62.7 1.0 copy-done.19
  63.7 0.9 copy-done.22
  64.6 0.9 copy-done.24
  65.6 0.9 copy-done.26
  66.5 7.9 %shard_map.129 = (bf16[768,1024]{1,0:T(8,128)(2,1)S(1)}, f32[768,16]{1,0:T(8,128)S(1)}, bf16[8,72,1024]{2,1,0:T(8,128)(2,1)S(1)}, f32[8,72,1024]{2,1,0:T(8,128)S(1)}) custom-call(s32[4]{0:T(128)S(1)} %copy-done.9, s32[1]{0:T(128)} %bitcast.core, f32[16,48,128]{2,1,0:T(8,128)S(1)} %all-to-all-done.1.stats, bf16[1024,384]{1,0:T(8,128)(2,1)S(1)} %copy-done.17, ...), custom_call_target="tpu_custom_call" | custom-call | flops 4000000000 | bytes 16000000 | tf_op jit(solution)/shard_map/pallas_call | solution.py:343
  74.4 0.0 copy-start.10
  74.4 0.1 collective-permute-start
  74.5 2.8 %collective-permute-done = bf16[8,72,1024]{2,1,0:T(8,128)(2,1)S(1)} collective-permute-done((bf16[8,72,1024]{2,1,0:T(8,128)(2,1)S(1)}, bf16[8,72,1024]{2,1,0:T(8,128)(2,1)S(1)}, u32[]{:S(2)}, u32[]{:S(2)}) %collective-permute-start) | collective-permute-done | bytes 1179680 | tf_op jit(solution)/shard_map/ppermute | solution.py:359
  77.3 0.4 add_convert_fusion
  77.8 21.8 %all_to_all.28.got = bf16[8,72,1024]{2,1,0:T(8,128)(2,1)S(1)} all-to-all(bf16[8,72,1024]{2,1,0:T(8,128)(2,1)S(1)} %add_convert_fusion), channel_id=1, replica_groups={{0,2,4,6,8,10,12,14},{1,3,5,7,9,11,13,15},{16,18,20,22,24,26,28,30},{17..., dimensions={0} | all-to-all | bytes 2359296 | tf_op jit(solution)/shard_map/all_to_all | solution.py:362
  99.6 0.3 shard_map.131
  99.8 15.8 %all_to_all.29.got = bf16[16,8,1024]{2,1,0:T(8,128)(2,1)S(1)} all-to-all(bf16[16,8,1024]{2,1,0:T(8,128)(2,1)S(1)} %shard_map.131), channel_id=1, replica_groups=mesh['chan'=16,'patch'=16] {'chan'}, dimensions={0} | all-to-all | bytes 524288 | tf_op jit(solution)/shard_map/all_to_all | solution.py:373
  115.7 0.8 shard_map.132
  116.4 3.5 %all-to-all-start.4 = ((f32[16,4,1024]{2,1,0:T(4,128)}), f32[16,4,1024]{2,1,0:T(4,128)S(1)}, u32[]{:S(2)}, u32[]{:S(2)}) async-start(f32[16,4,1024]{2,1,0:T(4,128)} %get-tuple-element.42), calls=%async_computation.4 | async-start | bytes 524288 | tf_op jit(solution)/shard_map/all_to_all | solution.py:377
  120.0 0.0 copy-start.11
  120.0 1.4 %copy-done.11 = bf16[768,1024]{1,0:T(8,128)(2,1)S(1)} copy-done((bf16[768,1024]{1,0:T(8,128)(2,1)S(1)}, bf16[768,1024]{1,0:T(8,128)(2,1)}, u32[]{:S(2)}) %copy-start.11) | copy-done | bytes 1572888
  121.4 3.6 %shard_map.130 = bf16[4,192,1024]{2,1,0:T(8,128)(2,1)} custom-call(bf16[768,1024]{1,0:T(8,128)(2,1)S(1)} %copy-done.11, f32[768,16]{1,0:T(8,128)S(1)} %get-tuple-element.36.score_grad, bf16[1024,1024]{1,0:T(8,128)(2,1)S(1)} %copy-done.5, bf16[1024,48]{1,0:T(8,128)(2,1)S(1)} %get-tuple-element.37.fold_one), custom_call_target="tpu_custom_call" | custom-call | flops 2000000000 | bytes 6000000 | tf_op jit(solution)/shard_map/pallas_call | solution.py:363
  125.0 1.2 shard_map.133
  126.1 6.0 %all-to-all-done.4 = f32[16,4,1024]{2,1,0:T(4,128)S(1)} async-done(((f32[16,4,1024]{2,1,0:T(4,128)}), f32[16,4,1024]{2,1,0:T(4,128)S(1)}, u32[]{:S(2)}, u32[]{:S(2)}) %all-to-all-start.4) | async-done | bytes 262176 | tf_op jit(solution)/shard_map/all_to_all | solution.py:377
  132.1 0.8 reshape.37
  (27 shorter events, 0.0 us)
Async XLA Ops:
  0.6 12.1 %copy-start.9 = (s32[4]{0:T(128)S(1)}, s32[4]{0:T(128)}, u32[]{:S(2)}) copy-start(s32[4]{0:T(128)} %table.3) | copy-start | bytes 52
  0.6 12.1 %copy-start.8 = (f32[1024]{0:T(1024)S(1)}, f32[1024]{0:T(1024)}, u32[]{:S(2)}) copy-start(f32[1024]{0:T(1024)} %param.14) | copy-start | bytes 12292
  0.7 12.1 %copy-start.7 = (f32[1024]{0:T(1024)S(1)}, f32[1024]{0:T(1024)}, u32[]{:S(2)}) copy-start(f32[1024]{0:T(1024)} %param.12) | copy-start | bytes 12292
  0.7 12.1 %copy-start.6 = (bf16[4,192,1024]{2,1,0:T(8,128)(2,1)S(1)}, bf16[4,192,1024]{2,1,0:T(8,128)(2,1)}, u32[]{:S(2)}) copy-start(bf16[4,192,1024]{2,1,0:T(8,128)(2,1)} %tok.1) | copy-start | bytes 4718596
  2.4 29.0 %all-to-all-start = ((bf16[16,12,1024]{2,1,0:T(8,128)(2,1)}), bf16[16,12,1024]{2,1,0:T(8,128)(2,1)S(1)}, u32[]{:S(2)}, u32[]{:S(2)}) async-start(bf16[16,12,1024]{2,1,0:T(8,128)(2,1)} %broadcast_in_dim.8), calls=%async_computation | async-start | bytes 1048576 | tf_op jit(solution)/shard_map/all_to_all | solution.py:302
  12.8 1.6 %copy-start = (bf16[1024,1024]{1,0:T(8,128)(2,1)S(1)}, bf16[1024,1024]{1,0:T(8,128)(2,1)}, u32[]{:S(2)}) copy-start(bf16[1024,1024]{1,0:T(8,128)(2,1)} %w_key.3) | copy-start | bytes 6291460
  14.4 1.6 %copy-start.2 = (bf16[1024,1024]{1,0:T(8,128)(2,1)S(1)}, bf16[1024,1024]{1,0:T(8,128)(2,1)}, u32[]{:S(2)}) copy-start(bf16[1024,1024]{1,0:T(8,128)(2,1)} %w_key_two.3) | copy-start | bytes 6291460
  15.9 1.6 %copy-start.4 = (bf16[1024,1024]{1,0:T(8,128)(2,1)S(1)}, bf16[1024,1024]{1,0:T(8,128)(2,1)}, u32[]{:S(2)}) copy-start(bf16[1024,1024]{1,0:T(8,128)(2,1)} %w_value.3) | copy-start | bytes 6291460
  25.0 1.1 copy-start.12
  26.2 0.9 copy-start.14
  27.0 0.9 copy-start.16
  27.9 0.7 copy-start.20
  28.6 2.9 %copy-start.25 = (bf16[1024,48]{1,0:T(8,128)(2,1)}, bf16[1024,48]{1,0:T(8,128)(2,1)S(1)}, u32[]{:S(2)}) copy-start(bf16[1024,48]{1,0:T(8,128)(2,1)S(1)} %get-tuple-element.34.fold_two) | copy-start | bytes 294916
  28.6 6.3 %copy-start.18 = (f32[768,16]{1,0:T(8,128)}, f32[768,16]{1,0:T(8,128)S(1)}, u32[]{:S(2)}) copy-start(f32[768,16]{1,0:T(8,128)S(1)} %get-tuple-element.33.weights) | copy-start | bytes 147460
  31.5 1.1 copy-start.15
  32.6 0.9 copy-start.21
  33.5 25.0 %copy-start.1 = (bf16[1024,1024]{1,0:T(8,128)(2,1)S(1)}, bf16[1024,1024]{1,0:T(8,128)(2,1)}, u32[]{:S(2)}) copy-start(bf16[1024,1024]{1,0:T(8,128)(2,1)} %w_key.3) | copy-start | bytes 6291460
  35.0 0.7 copy-start.23
  35.6 22.9 %all-to-all-start.1 = ((f32[16,48,128]{2,1,0:T(8,128)}), f32[16,48,128]{2,1,0:T(8,128)S(1)}, u32[]{:S(2)}, u32[]{:S(2)}) async-start(f32[16,48,128]{2,1,0:T(8,128)} %get-tuple-element.28), calls=%async_computation.1 | async-start | bytes 786432 | tf_op jit(solution)/shard_map/all_to_all | solution.py:340
  58.6 1.6 %copy-start.3 = (bf16[1024,1024]{1,0:T(8,128)(2,1)S(1)}, bf16[1024,1024]{1,0:T(8,128)(2,1)}, u32[]{:S(2)}) copy-start(bf16[1024,1024]{1,0:T(8,128)(2,1)} %w_key_two.3) | copy-start | bytes 6291460
  60.2 1.4 %copy-start.13 = (bf16[1024,768]{1,0:T(8,128)(2,1)S(1)}, bf16[1024,768]{1,0:T(8,128)(2,1)}, u32[]{:S(2)}) copy-start(bf16[1024,768]{1,0:T(8,128)(2,1)} %copy-done.12) | copy-start | bytes 4718596
  61.6 1.1 copy-start.17
  62.7 1.0 copy-start.19
  63.7 0.9 copy-start.22
  64.6 0.9 copy-start.24
  65.6 0.9 copy-start.26
  74.4 3.4 %copy-start.10 = (bf16[768,1024]{1,0:T(8,128)(2,1)}, bf16[768,1024]{1,0:T(8,128)(2,1)S(1)}, u32[]{:S(2)}) copy-start(bf16[768,1024]{1,0:T(8,128)(2,1)S(1)} %get-tuple-element.35.value_grad) | copy-start | bytes 4718596
  74.4 2.9 %collective-permute-start = (bf16[8,72,1024]{2,1,0:T(8,128)(2,1)S(1)}, bf16[8,72,1024]{2,1,0:T(8,128)(2,1)S(1)}, u32[]{:S(2)}, u32[]{:S(2)}) collective-permute-start(bf16[8,72,1024]{2,1,0:T(8,128)(2,1)S(1)} %get-tuple-element.39), channel_id=1, source_target_pairs={{0,1},{1,0},{2,3},{3,2},{4,5},{5,4},{6,7},{7,6},{8,9},{9,8},{10,11... | collective-permute-start | bytes 3538952 | tf_op jit(solution)/shard_map/ppermute | solution.py:359
  99.6 20.4 %copy-start.5 = (bf16[1024,1024]{1,0:T(8,128)(2,1)S(1)}, bf16[1024,1024]{1,0:T(8,128)(2,1)}, u32[]{:S(2)}) copy-start(bf16[1024,1024]{1,0:T(8,128)(2,1)} %w_value.3) | copy-start | bytes 6291460
  116.4 15.7 %all-to-all-start.4 = ((f32[16,4,1024]{2,1,0:T(4,128)}), f32[16,4,1024]{2,1,0:T(4,128)S(1)}, u32[]{:S(2)}, u32[]{:S(2)}) async-start(f32[16,4,1024]{2,1,0:T(4,128)} %get-tuple-element.42), calls=%async_computation.4 | async-start | bytes 524288 | tf_op jit(solution)/shard_map/all_to_all | solution.py:377
  120.0 1.4 %copy-start.11 = (bf16[768,1024]{1,0:T(8,128)(2,1)S(1)}, bf16[768,1024]{1,0:T(8,128)(2,1)}, u32[]{:S(2)}) copy-start(bf16[768,1024]{1,0:T(8,128)(2,1)} %copy-done.10) | copy-start | bytes 4718596

commit v2 on v1

--- a/solution.py
+++ b/solution.py
@@ -19,10 +19,11 @@
 NB = ROWS // BLK
 TOK = CH * BLK
 AGG = GR * BLK
+PAIRS = HEADS * HEADS
 SLAB = 72
 F32 = jnp.float32
 BF16 = jnp.bfloat16
-LIMIT = 40 * 2**20
+MIB = 2**20
 
 
 def nn(a, b):
@@ -129,11 +130,19 @@
     return jnp.concatenate([x[:, HEADS * k : HEADS * (k + 1)] for k in range(8)], 0)
 
 
-def stats_kernel(agg, cot, scores_two, dw_two, stats):
+def tile_kernel(cot, out):
+    for k in range(16):
+        out[k] = cot[0]
+
+
+def stats_kernel(agg, got, scores_two, dw_two, stats, cot, rows_f):
     heads = spread(1)
+    for k in range(16):
+        rows_f[12 * k : 12 * k + 12] = got[k].astype(F32)
+    cot[...] = rows_f[...].astype(BF16)
     score, grad = [[], []], [[], []]
     for b in range(NB):
-        cot_f = cot[b * BLK : (b + 1) * BLK].astype(F32)
+        cot_f = rows_f[b * BLK : (b + 1) * BLK]
         for g in range(GR):
             rows = slice(b * AGG + g * BLK, b * AGG + (g + 1) * BLK)
             dw = head_sum(agg[rows].astype(F32) * cot_f, heads)
@@ -152,83 +161,160 @@
         stats[k] = both
 
 
-def backward_kernel(
-    table, core, stats, agg_t, tok_t, cot, scores_two, dw_two, values, weights,
-    w_key, w_key_two, fold_two,
-    value_grad, score_grad, send, keep, sums,
+def pre_kernel(values, cot, fold_two, direct, cross):
+    heads = spread(1)
+    row = lax.broadcasted_iota(jnp.int32, (HEADS, PAIRS), 0)
+    col = lax.broadcasted_iota(jnp.int32, (HEADS, PAIRS), 1)
+    copies = jnp.where(row == (col & (HEADS - 1)), 1.0, 0.0).astype(BF16)
+    own = (lax.broadcasted_iota(jnp.int32, (D, PAIRS), 0) >> SHIFT) == (
+        lax.broadcasted_iota(jnp.int32, (D, PAIRS), 1) >> 4
+    )
+    wide = [
+        jnp.where(own, nn(fold_two[:, k * HEADS : (k + 1) * HEADS], copies), 0.0).astype(BF16)
+        for k in range(2)
+    ]
+    for b in range(NB):
+        trows = slice(b * TOK, (b + 1) * TOK)
+        cot_f = cot[b * BLK : (b + 1) * BLK].astype(F32)
+        vals = values[trows]
+        direct[trows] = head_sum(jnp.concatenate([cot_f] * CH, 0) * vals, heads)
+        high, low = split2(vals)
+        cross[trows] = nn(high, wide[0]) + nn(high, wide[1]) + nn(low, wide[0])
+
+
+def back_kernel(
+    table, core, stats, cot_h, scores_h, dw_h, weights_h, fold_h, direct_h, cross_h, tok_h, agg_h,
+    key_h, key_two_h,
+    value_grad, score_grad_h, send_h, keep_h,
+    cot, scores_two, dw_two, weights, fold_two, direct, cross, tok_t, agg_t, w_key, w_key_two,
+    grad, sums, send, keep, score_grad, sems,
 ):
+    sources = (
+        cot_h, scores_h, dw_h, weights_h, fold_h, tok_h, direct_h, cross_h, agg_h, key_h, key_two_h,
+    )
+    targets = (
+        cot, scores_two, dw_two, weights, fold_two, tok_t, direct, cross, agg_t, w_key, w_key_two,
+    )
+    copies = [
+        pltpu.make_async_copy(x, y, sems.at[k]) for k, (x, y) in enumerate(zip(sources, targets))
+    ]
+    for c in copies[:5]:
+        c.start()
     heads, heads2 = spread(1), spread(2)
     group = [table[c] for c in range(CH)]
+
+    def by_channel(x):
+        return jnp.concatenate(
+            [jnp.where(group[c] == 0, x[:BLK], x[BLK:]) for c in range(CH)], 0
+        )
+
     logs = stats[:, :24, :]
     top = jnp.max(logs, 0)
     expo = jnp.exp(logs - top[None])
     total = jnp.sum(expo, 0)
     inner = unpack(jnp.sum(expo * stats[:, 24:, :], 0) / total)
     log_total = unpack(top + jnp.log(total))
-    grads_two = []
+    for c in copies[:5]:
+        c.wait()
+    for c in copies[5:]:
+        c.start()
+    w_two, s_two = [], []
     for b in range(NB):
         rows = slice(b * BLK, (b + 1) * BLK)
         arows = slice(b * AGG, (b + 1) * AGG)
         trows = slice(b * TOK, (b + 1) * TOK)
         twice = lambda x: jnp.concatenate([x, x], 0)
-        w_two = jnp.exp(scores_two[arows] - twice(log_total[rows]))
-        s_two = w_two * (dw_two[arows] - twice(inner[rows]))
-        grads_two.append(s_two)
+        w_now = jnp.exp(scores_two[arows] - twice(log_total[rows]))
+        s_now = w_now * (dw_two[arows] - twice(inner[rows]))
+        w_two.append(w_now)
+        s_two.append(s_now)
         cot_f = cot[rows].astype(F32)
-        agg_grad = expand(w_two, heads2) * twice(cot_f) + folded_back(s_two, fold_two[...])
-        agg_grad = agg_grad.astype(BF16).astype(F32)
-        first, second = agg_grad[:BLK], agg_grad[BLK:]
-        chan = jnp.concatenate([jnp.where(group[c] == 0, first, second) for c in range(CH)], 0)
+        agg_grad = expand(w_now, heads2) * twice(cot_f) + folded_back(s_now, fold_two[...])
+        grad[trows] = (expand(weights[trows], heads2) * by_channel(agg_grad)).astype(BF16)
+    copies[5].wait()
+    for n in range(4):
+        cols = slice(n * 256, (n + 1) * 256)
+        out = nn(tok_t[...], grad[:, cols])
+        for p in range(16):
+            sums[p * SLAB : p * SLAB + 64, cols] = out[p * 64 : (p + 1) * 64]
+    row = lax.broadcasted_iota(jnp.int32, (2 * HEADS, PAIRS), 0) & (HEADS - 1)
+    col = lax.broadcasted_iota(jnp.int32, (2 * HEADS, PAIRS), 1)
+    tiled = jnp.where(row == (col & (HEADS - 1)), 1.0, 0.0).astype(BF16)
+    gather = jnp.where(row == (col >> 4), 1.0, 0.0).astype(BF16)[:HEADS]
+    copies[6].wait()
+    copies[7].wait()
+    for b in range(NB):
+        trows = slice(b * TOK, (b + 1) * TOK)
+        score = by_channel(s_two[b])
+        product = nn(jnp.concatenate(split2(score), 1), tiled) * cross[trows]
+        high, low = split2(product)
+        dw = by_channel(w_two[b]) * direct[trows] + nt(high, gather) + nt(low, gather)
         weight = weights[trows]
-        value_grad[trows] = (expand(weight, heads2) * chan).astype(BF16)
-        dw = head_sum(chan * values[trows], heads)
         wdw = weight * dw
         part = [wdw[c * BLK : (c + 1) * BLK] for c in range(CH)]
-        inner_one = [
-            sum(jnp.where(group[c] == g, part[c], 0.0) for c in range(CH)) for g in range(GR)
-        ]
         own = jnp.concatenate(
-            [jnp.where(group[c] == 0, inner_one[0], inner_one[1]) for c in range(CH)], 0
+            [sum(jnp.where(group[c] == g, part[c], 0.0) for c in range(CH)) for g in range(GR)], 0
         )
-        score_grad[trows] = weight * (dw - own)
-    for n in range(4):
-        cols = slice(n * 256, (n + 1) * 256)
-        out = nn(tok_t[...], value_grad[:, cols])
-        for p in range(16):
-            sums[p * SLAB : p * SLAB + 64, cols] = out[p * 64 : (p + 1) * 64]
+        score_grad[trows] = weight * (dw - by_channel(own))
 
     def outer(left, right):
         both = nn(left, jnp.concatenate(split2(right), 1))
         return both[:, :HEADS] + both[:, HEADS:]
 
+    started = [
+        pltpu.make_async_copy(grad, value_grad, sems.at[11]),
+        pltpu.make_async_copy(score_grad, score_grad_h, sems.at[14]),
+    ]
+    for c in started:
+        c.start()
     ones = outer(tok_t[...], score_grad[...])
-    twos = outer(agg_t[...], jnp.concatenate(grads_two, 0))
-    grads = jnp.concatenate([ones, twos, jnp.zeros((D, 128 - 2 * HEADS), F32)], 1).T
+    copies[8].wait()
+    twos = outer(agg_t[...], jnp.concatenate(s_two, 0))
+    grads = jnp.concatenate([ones, twos, jnp.zeros((D, 128 - 2 * HEADS), F32)], 1).T[: 2 * HEADS]
     lines = []
+    copies[9].wait()
+    copies[10].wait()
     for k, weight in enumerate((w_key, w_key_two)):
         high, low = split2(grads[k * HEADS : (k + 1) * HEADS])
         out = nn(jnp.concatenate([high, low], 0), weight[...])
         out = (out[:HEADS] + out[HEADS:]) * heads.astype(F32)
         lines.append(jnp.sum(out, 0, keepdims=True) * SCALE)
-    quads = jnp.concatenate(
-        [lines[0][:, :512], lines[0][:, 512:], lines[1][:, :512], lines[1][:, 512:]], 0
-    )
-    high = quads.astype(BF16).astype(F32)
-    small = jnp.concatenate([high, quads - high], 0)
-    turned = jnp.concatenate([grads[: 2 * HEADS, 64:], grads[: 2 * HEADS, :64]], 1)
+    quarters = jnp.concatenate(
+        [line[:, k * 256 : (k + 1) * 256] for line in lines for k in range(4)], 0
+    )
+    left = (lax.broadcasted_iota(jnp.int32, (8, D), 1) & 64) == 0
+    pairs = []
+    for odd in range(2):
+        for k in range(2):
+            one, two = grads[16 * k : 16 * k + 8], grads[16 * k + 8 : 16 * k + 16]
+            if odd:
+                one = jnp.concatenate([one[:, 64:], one[:, :64]], 1)
+            else:
+                two = jnp.concatenate([two[:, D - 64 :], two[:, : D - 64]], 1)
+            pairs.append(jnp.where(left, one, two))
     for p in range(16):
-        source = turned if p % 2 else grads
         rows = slice(p * SLAB + 64, (p + 1) * SLAB)
         lanes = slice((p // 2) * 128, (p // 2 + 1) * 128)
-        for k in range(4):
-            sums[rows, k * 128 : (k + 1) * 128] = source[8 * k : 8 * k + 8, lanes]
-        sums[rows, 512:] = small
+        for half in (0, 512):
+            for k in range(2):
+                spot = slice(half + k * 128, half + (k + 1) * 128)
+                sums[rows, spot] = pairs[2 * (p % 2) + k][:, lanes]
+            sums[rows, half + 256 : half + 512] = quarters
     mine = core[0]
-    for k in range(8):
-        away = pl.multiple_of((2 * k + 1 - mine) * SLAB, 8)
-        here = pl.multiple_of((2 * k + mine) * SLAB, 8)
-        send[k] = sums[pl.ds(away, SLAB), :].astype(BF16)
-        keep[k] = sums[pl.ds(here, SLAB), :]
+    for which, (held, target) in enumerate(((send, send_h), (keep, keep_h))):
+        side = mine if which else 1 - mine
+        for k in range(8):
+            slab = sums[pl.ds(pl.multiple_of((2 * k + side) * SLAB, 8), SLAB), :]
+            for half in range(2):
+                held[8 * half + k] = slab[:, half * 512 : (half + 1) * 512].astype(held.dtype)
+        started.append(pltpu.make_async_copy(held, target, sems.at[12 + which]))
+        started[-1].start()
+    for c in started:
+        c.wait()
+
+
+def pair_kernel(keep, got, out):
+    out[...] = (keep[...].astype(F32) + got[...].astype(F32)).astype(BF16)
 
 
 def token_kernel(value_grad, score_grad, w_value, fold_one, out):
@@ -238,41 +324,42 @@
 
 def rows_kernel(got, out):
     total = got[0].astype(F32)
+    for k in range(1, 16):
+        total = total + got[k].astype(F32)
+    total = total.astype(BF16)
+    for z in range(8):
+        out[z] = jnp.concatenate([total[8 * z : 8 * z + 8], total[64:]], 1)
+
+
+def chans_kernel(got, rows, extra):
+    total = got[0].astype(F32)
     for k in range(1, 8):
         total = total + got[k].astype(F32)
-    extra = total[64:]
-    tall = [extra[:, k * 128 : k * 128 + 64] for k in range(4)]
-    line = extra[:4, 512:] + extra[4:, 512:]
-    extra = jnp.concatenate([t[:4] for t in tall] + [t[4:] for t in tall] + [line], 1)
+    own = total[:, :512].astype(BF16)
     for c in range(16):
-        out[c] = jnp.concatenate([total[4 * c : 4 * c + 4], extra], 0).astype(BF16)
-
-
-def chans_kernel(got, rows, extra):
-    total = got[0].astype(F32)
-    for k in range(1, 16):
-        total = total + got[k].astype(F32)
-    for c in range(16):
-        rows[c] = total[:4]
-    extra[...] = total[4:]
+        rows[c] = own
+    extra[...] = total[:, 512:]
+
+
+def last_kernel(got, out):
+    for r in range(8):
+        for half in range(2):
+            out[8 * r : 8 * r + 8, half * 512 : (half + 1) * 512] = got[2 * r + half].astype(F32)
 
 
 def small_kernel(extra, query_one, query_two, grad_key, grad_key_two, line_one, line_two):
     x = extra[...]
-    tall = [x[:, k * 64 : (k + 1) * 64] for k in range(8)]
-    grads = jnp.concatenate(
-        [jnp.concatenate([tall[k], tall[k + 4]], 0) for k in range(4)], 0
-    )
-    grads = jnp.concatenate([grads, jnp.zeros((32, 64), F32)], 0)
-    turned = jnp.concatenate([grads, jnp.zeros((64, 64), F32)], 1).T[:64]
+    grads = jnp.concatenate([x[:, k * 64 : (k + 1) * 64] for k in range(4)], 0)
+    grads = jnp.concatenate([grads, jnp.zeros((96, 64), F32)], 0)
+    turned = jnp.concatenate([grads, jnp.zeros((128, 64), F32)], 1).T[:64]
     heads3 = spread(3)
     for k, (query, out) in enumerate(((query_one, grad_key), (query_two, grad_key_two))):
         part = turned[:, k * HEADS : (k + 1) * HEADS]
         out[...] = nn(jnp.concatenate(split3(part), 1), heads3) * (query[...] * SCALE)
-    line_one[:, :512] = x[0:1, 512:]
-    line_one[:, 512:] = x[1:2, 512:]
-    line_two[:, :512] = x[2:3, 512:]
-    line_two[:, 512:] = x[3:4, 512:]
+    for k in range(4):
+        cols = slice(k * 256, (k + 1) * 256)
+        line_one[:, cols] = x[k : k + 1, 256:]
+        line_two[:, cols] = x[4 + k : 5 + k, 256:]
 
 
 def shape(dims, dtype):
@@ -286,11 +373,11 @@
     return pl.BlockSpec(dims, lambda i: (0,) * len(dims))
 
 
-def call(kernel, out_shape, flops, nbytes, **kw):
+def call(kernel, out_shape, flops, nbytes, limit=60, **kw):
     return pl.pallas_call(
         kernel,
         out_shape=out_shape,
-        compiler_params=pltpu.CompilerParams(vmem_limit_bytes=LIMIT),
+        compiler_params=pltpu.CompilerParams(vmem_limit_bytes=limit * MIB),
         cost_estimate=pl.CostEstimate(flops=flops, bytes_accessed=nbytes, transcendentals=0),
         **kw,
     )
@@ -298,7 +385,7 @@
 
 def shards(tokens, table, w_key, w_value, query_one, w_key_two, query_two, cotangent):
     query_one, query_two = query_one.reshape(1, D), query_two.reshape(1, D)
-    tiled = jnp.broadcast_to(cotangent, (16, ROWS // 16, D)).reshape(ROWS, D)
+    tiled = call(tile_kernel, shape((16, ROWS // 16, D), BF16), 10**4, 10**6, 4)(cotangent)
     cot = lax.all_to_all(tiled, "chan", 0, 0, tiled=True)
     full = whole((D, D))
     by_rows = lambda n, w: pl.BlockSpec((n, w), lambda i: (i, 0))
@@ -331,60 +418,98 @@
             whole((D, 3 * HEADS)),
         ),
     )(table, tokens, w_value, w_key, w_key_two, query_one, query_two)
-    dw_two, stats = call(
+    dw_two, stats, cot = call(
         stats_kernel,
-        (shape((NB * AGG, HEADS), F32), shape((16, 48, 128), F32)),
+        (shape((NB * AGG, HEADS), F32), shape((16, 48, 128), F32), shape((ROWS, D), BF16)),
         10**9,
         2 * 10**6,
+        scratch_shapes=[pltpu.VMEM((ROWS, D), F32)],
     )(agg, cot, scores_two)
+    stats, fold_now = lax.optimization_barrier((stats, fold_two))
     stats = lax.all_to_all(stats, "chan", 0, 0, tiled=True)
     core = lax.rem(lax.axis_index("patch"), 2).astype(jnp.int32).reshape(1)
+    direct, cross = call(
+        pre_kernel,
+        (shape((NB * TOK, HEADS), F32), shape((NB * TOK, PAIRS), F32)),
+        10**9,
+        5 * 10**6,
+    )(values, cot, fold_now)
     vmem = pl.BlockSpec(memory_space=pltpu.VMEM)
+    hbm = pl.BlockSpec(memory_space=pltpu.HBM)
+    fetched = (
+        cot, scores_two, dw_two, weights, fold_two, direct, cross, tok_t, agg_t, w_key, w_key_two,
+    )
     value_grad, score_grad, send, keep = call(
-        backward_kernel,
+        back_kernel,
         (
             shape((NB * TOK, D), BF16),
             shape((NB * TOK, HEADS), F32),
-            shape((8, SLAB, D), BF16),
-            shape((8, SLAB, D), F32),
+            shape((16, SLAB, 512), BF16),
+            shape((16, SLAB, 512), BF16),
         ),
         4 * 10**9,
         16 * 10**6,
-        in_specs=[SMEM, SMEM] + [vmem] * 11,
-        scratch_shapes=[pltpu.VMEM((16 * SLAB, D), F32)],
-    )(
-        table, core, stats, agg_t, tok_t, cot, scores_two, dw_two, values, weights,
-        w_key, w_key_two, fold_two,
-    )
+        in_specs=[SMEM, SMEM, vmem] + [hbm] * len(fetched),
+        out_specs=(hbm, hbm, hbm, hbm),
+        scratch_shapes=[pltpu.VMEM(x.shape, x.dtype) for x in fetched]
+        + [
+            pltpu.VMEM((NB * TOK, D), BF16),
+            pltpu.VMEM((16 * SLAB, D), F32),
+            pltpu.VMEM((16, SLAB, 512), BF16),
+            pltpu.VMEM((16, SLAB, 512), BF16),
+            pltpu.VMEM((NB * TOK, HEADS), F32),
+            pltpu.SemaphoreType.DMA((15,)),
+        ],
+    )(table, core, stats, *fetched)
     got = lax.ppermute(send, "patch", [(i, i ^ 1) for i in range(16)])
-    pairs = (keep + got.astype(F32)).astype(BF16)
-    same_core = [[i for i in range(16) if i % 2 == k] for k in range(2)]
-    got = lax.all_to_all(pairs, "patch", 0, 0, tiled=True, axis_index_groups=same_core)
+    slabs = pl.BlockSpec((4, SLAB, 512), lambda i: (i, 0, 0))
+    pairs = call(
+        pair_kernel,
+        shape((16, SLAB, 512), BF16),
+        10**6,
+        5 * 10**6,
+        12,
+        grid=(4,),
+        in_specs=[slabs, slabs],
+        out_specs=slabs,
+    )(keep, got)
+    planes = [
+        [(2 * z + h) * 16 + 2 * k + core_bit for h in range(2) for k in range(8)]
+        for z in range(8)
+        for core_bit in range(2)
+    ]
+    got = lax.all_to_all(
+        pairs, ("chan", "patch"), 0, 0, tiled=True, axis_index_groups=planes
+    )
     token_grad = call(
         token_kernel,
         shape((CH, ROWS, D), BF16),
         2 * 10**9,
         6 * 10**6,
+        24,
         grid=(NB,),
         in_specs=[by_rows(TOK, D), by_rows(TOK, HEADS), full, whole((D, 3 * HEADS))],
         out_specs=token_spec,
     )(value_grad, score_grad, w_value, fold_one)
-    rows = call(rows_kernel, shape((16, 8, D), BF16), 10**6, 2 * 10**6)(got)
-    rows = lax.all_to_all(rows, "chan", 0, 0, tiled=True)
+    rows = call(rows_kernel, shape((8, 8, D), BF16), 10**6, 2 * 10**6, 8)(got)
+    same_half = [[2 * z + h for z in range(8)] for h in range(2)]
+    rows = lax.all_to_all(rows, "chan", 0, 0, tiled=True, axis_index_groups=same_half)
     rows, extra = call(
-        chans_kernel, (shape((16, 4, D), F32), shape((4, D), F32)), 10**6, 10**6
+        chans_kernel, (shape((16, 8, 512), BF16), shape((8, 512), F32)), 10**6, 10**6, 8
     )(rows)
     rows = lax.all_to_all(rows, "chan", 0, 0, tiled=True)
+    grad_value = call(last_kernel, shape((64, D), F32), 10**6, 10**6, 8)(rows)
     grad_key, grad_key_two, line_one, line_two = call(
         small_kernel,
         (shape((64, D), F32), shape((64, D), F32), shape((1, D), F32), shape((1, D), F32)),
         10**8,
         10**6,
+        8,
     )(extra, query_one, query_two)
     return (
         token_grad,
         grad_key,
-        rows.reshape(64, D),
+        grad_value,
         grad_key_two,
         line_one.reshape(D),
         line_two.reshape(D),

time: 134 us -> 123 us (0.918)
  local copies, waits for them, and re-layouts: 23.1 us -> 4.98 us
  Pallas kernels: 22.5 us -> 37.7 us
  starting transfers between devices: 21.4 us -> 17.5 us
  blocking collectives: 37.6 us -> 34.6 us
    unnamed x54 -> x20, local copies, waits for them, and re-layouts: 20.5 us -> 4.98 us
    pallas_call x3 -> x7, Pallas kernels: 8.89 us -> 19.4 us  [the longest x1 11.3 us: shards(): call(back_kernel, (shape((NB * TOK, D), BF16), shape((NB * TOK, HEADS), F...]
    all_to_all x1, waiting for transfers between devices: 2.76 us -> 8.11 us  [shards(): cot = lax.all_to_all(tiled, 'chan', 0, 0, tiled=True)]
    all_to_all x1, waiting for transfers between devices: 15.5 us -> 10.4 us  [shards(): stats = lax.all_to_all(stats, 'chan', 0, 0, tiled=True)]
    all_to_all x1, starting transfers between devices: 7.45 us -> 3.55 us  [shards(): stats = lax.all_to_all(stats, 'chan', 0, 0, tiled=True)]
    pallas_call x1, Pallas kernels: 7.48 us -> 10.5 us  [shards(): call(forward_kernel, (shape((NB * TOK, D), F32), shape((NB * TOK, HEADS),...]
    all_to_all x2, blocking collectives: 37.6 us -> 34.6 us  [the longest x1 22.9 us: shards(): lax.all_to_all(pairs, ('chan', 'patch'), 0, 0, tiled=True, axis_index_gro...]
    broadcast_in_dim x1 -> x0, local copies, waits for them, and re-layouts: 1.74 us -> none  [shards(): tiled = jnp.broadcast_to(cotangent, (16, ROWS // 16, D)).reshape(ROWS, D)]
  transfers between devices with their start and end apart: 4 -> 4, of which waited for: 4 -> 4; matrix products, arithmetic and copies ran while one was open for 0% -> 0% of each run, Pallas kernels for 9% -> 17%
where the time goes in v2:
time: 123 us; the launch traced here: 122 us
  Pallas kernels  37.7 us (31%)
  blocking collectives  34.6 us (28%)
  waiting for transfers between devices  26.5 us (22%)
  starting transfers between devices  17.5 us (14%)
  local copies, waits for them, and re-layouts  4.98 us (4%)
    all_to_all x1, blocking collectives, shards(): lax.all_to_all(pairs, ('chan', 'patch'), 0, 0, tiled=True, axis_index_gro...  22.9 us
    all_to_all x1, blocking collectives, shards(): lax.all_to_all(rows, 'chan', 0, 0, tiled=True, axis_index_groups=same_half)  11.7 us
    pallas_call x1, Pallas kernels, shards(): call(back_kernel, (shape((NB * TOK, D), BF16), shape((NB * TOK, HEADS), F...  11.3 us
    pallas_call x1, Pallas kernels, shards(): call(forward_kernel, (shape((NB * TOK, D), F32), shape((NB * TOK, HEADS),...  10.5 us
    all_to_all x1, waiting for transfers between devices, shards(): stats = lax.all_to_all(stats, 'chan', 0, 0, tiled=True)  10.4 us
    all_to_all x1, starting transfers between devices, shards(): cot = lax.all_to_all(tiled, 'chan', 0, 0, tiled=True)  10.3 us
    all_to_all x1, waiting for transfers between devices, shards(): cot = lax.all_to_all(tiled, 'chan', 0, 0, tiled=True)  8.11 us
    pallas_call x1, Pallas kernels, shards(): call(pre_kernel, (shape((NB * TOK, HEADS), F32), shape((NB * TOK, PAIRS),...  5.4 us
  transfers between devices with their start and end apart: 4, of which 4 were waited for; matrix products, arithmetic and copies ran while one was open for 0% of the time, Pallas kernels for 17%

profile of v2, /device:TPU:8, one launch (start us, length us, event | category | flops | bytes accessed | tf_op | source)
XLA Modules:
  0.0 122.0 jit_solution(288876290063247678)
XLA Ops:
  0.6 0.0 copy-start.1
  0.6 0.7 copy-done.1
  1.4 0.8 shard_map.128
  2.2 10.3 %all-to-all-start = ((bf16[16,12,1024]{2,1,0:T(8,128)(2,1)}), bf16[16,12,1024]{2,1,0:T(8,128)(2,1)S(1)}, u32[]{:S(2)}, u32[]{:S(2)}) async-start(bf16[16,12,1024]{2,1,0:T(8,128)(2,1)} %shard_map.128), calls=%async_computation | async-start | bytes 1048576 | tf_op jit(solution)/shard_map/all_to_all | solution.py:389
  12.5 10.5 %shard_map.127 = (f32[768,1024]{1,0:T(8,128)}, f32[768,16]{1,0:T(8,128)}, bf16[384,1024]{1,0:T(8,128)(2,1)}, bf16[1024,384]{1,0:T(8,128)(2,1)}, bf16[1024,768]{1...) custom-call(s32[4]{0:T(128)} %table.3, bf16[4,192,1024]{2,1,0:T(8,128)(2,1)} %tok.1, ...), custom_call_target="tpu_custom_call" | custom-call | flops 4000000000 | bytes 16000000 | tf_op jit(solution)/shard_map/pallas_call | solution.py:394
  23.1 8.1 %all-to-all-done.got = bf16[16,12,1024]{2,1,0:T(8,128)(2,1)S(1)} async-done(((bf16[16,12,1024]{2,1,0:T(8,128)(2,1)}), bf16[16,12,1024]{2,1,0:T(8,128)(2,1)S(1)}, u32[]{:S(2)}, u32[]{:S(2)}) %all-to-all-start) | async-done | bytes 393248 | tf_op jit(solution)/shard_map/all_to_all | solution.py:389
  31.2 0.0 copy-start.8
  31.2 0.8 copy-done.8
  32.0 3.0 %shard_map.129 = (f32[384,16]{1,0:T(8,128)}, f32[16,48,128]{2,1,0:T(8,128)}, bf16[192,1024]{1,0:T(8,128)(2,1)}) custom-call(bf16[384,1024]{1,0:T(8,128)(2,1)} %get-tuple-element.31.agg, bf16[16,12,1024]{2,1,0:T(8,128)(2,1)} %copy-done.8, f32[384,16]{1,0:T(8,128)} %get-tuple-element.32.scores_two.scores_h), custom_call_target="tpu_custom_call" | custom-call | flops 1000000000 | bytes 2000000 | tf_op jit(solution)/shard_map/pallas_call | solution.py:421
  34.9 3.6 %all-to-all-start.1 = ((f32[16,48,128]{2,1,0:T(8,128)}), f32[16,48,128]{2,1,0:T(8,128)S(1)}, u32[]{:S(2)}, u32[]{:S(2)}) async-start(f32[16,48,128]{2,1,0:T(8,128)} %get-tuple-element.35), calls=%async_computation.1 | async-start | bytes 786432 | tf_op jit(solution)/shard_map/all_to_all | solution.py:429
  38.5 5.4 %shard_map.130 = (f32[768,16]{1,0:T(8,128)}, f32[768,256]{1,0:T(8,128)}) custom-call(f32[768,1024]{1,0:T(8,128)} %get-tuple-element.39.values, bf16[192,1024]{1,0:T(8,128)(2,1)} %get-tuple-element.36.cot.cot_h, bf16[1024,48]{1,0:T(8,128)(2,1)} %get-tuple-element.40.fold_two.fold_h), custom_call_target="tpu_custom_call" | custom-call | flops 1000000000 | bytes 5000000 | tf_op jit(solution)/shard_map/pallas_call | solution.py:431
  43.9 10.4 %all-to-all-done.1.stats = f32[16,48,128]{2,1,0:T(8,128)S(1)} async-done(((f32[16,48,128]{2,1,0:T(8,128)}), f32[16,48,128]{2,1,0:T(8,128)S(1)}, u32[]{:S(2)}, u32[]{:S(2)}) %all-to-all-start.1) | async-done | bytes 393248 | tf_op jit(solution)/shard_map/all_to_all | solution.py:429
  54.3 0.0 copy-start.9
  54.3 0.7 copy-done.9
  55.1 11.3 %shard_map.131 = (bf16[768,1024]{1,0:T(8,128)(2,1)}, f32[768,16]{1,0:T(8,128)}, bf16[16,72,512]{2,1,0:T(8,128)(2,1)}, bf16[16,72,512]{2,1,0:T(8,128)(2,1)}) custom-call(s32[4]{0:T(128)} %table.3, s32[1]{0:T(128)} %bitcast.core, f32[16,48,128]{2,1,0:T(8,128)} %copy-done.9, bf16[192,1024]{1,0:T(8,128)(2,1)} %get-tuple-element.36.cot.cot_h, ...), custom_call_target="tpu_custom_call" | custom-call | flops 4000000000 | bytes 16000000 | tf_op jit(solution)/shard_map/pallas_call | solution.py:442
  66.4 0.1 collective-permute-start
  66.5 3.0 %collective-permute-done.got = bf16[16,72,512]{2,1,0:T(8,128)(2,1)S(1)} collective-permute-done((bf16[16,72,512]{2,1,0:T(8,128)(2,1)}, bf16[16,72,512]{2,1,0:T(8,128)(2,1)S(1)}, u32[]{:S(2)}, u32[]{:S(2)}) %collective-permute-start) | collective-permute-done | bytes 1179680 | tf_op jit(solution)/shard_map/ppermute | solution.py:464
  69.5 0.0 copy-start
  69.5 1.3 %copy-done = bf16[16,72,512]{2,1,0:T(8,128)(2,1)S(1)} copy-done((bf16[16,72,512]{2,1,0:T(8,128)(2,1)S(1)}, bf16[16,72,512]{2,1,0:T(8,128)(2,1)}, u32[]{:S(2)}) %copy-start) | copy-done | bytes 1179672
  70.8 0.3 shard_map.133
  71.1 0.0 copy-start.2
  71.1 22.9 %all_to_all.25.got = bf16[16,72,512]{2,1,0:T(8,128)(2,1)S(1)} all-to-all(bf16[16,72,512]{2,1,0:T(8,128)(2,1)S(1)} %shard_map.133), channel_id=1, replica_groups={{0,2,4,6,8,10,12,14,16,18,20,22,24,26,28,30},{1,3,5,7,9,11,13,15,17,19,..., dimensions={0} | all-to-all | bytes 2359296 | tf_op jit(solution)/shard_map/all_to_all | solution.py:481
  94.1 0.0 copy-start.6
  94.1 0.0 copy-start.7
  94.1 0.2 shard_map.134
  94.2 11.7 %all_to_all.26.got = bf16[8,8,1024]{2,1,0:T(8,128)(2,1)S(1)} all-to-all(bf16[8,8,1024]{2,1,0:T(8,128)(2,1)S(1)} %shard_map.134), channel_id=1, replica_groups={{0,32,64,96,128,160,192,224},{16,48,80,112,144,176,208,240},{1,33,65,97..., dimensions={0} | all-to-all | bytes 262144 | tf_op jit(solution)/shard_map/all_to_all | solution.py:496
  106.0 0.7 shard_map.135
  106.6 3.5 %all-to-all-start.4 = ((bf16[16,8,512]{2,1,0:T(8,128)(2,1)}), bf16[16,8,512]{2,1,0:T(8,128)(2,1)S(1)}, u32[]{:S(2)}, u32[]{:S(2)}) async-start(bf16[16,8,512]{2,1,0:T(8,128)(2,1)} %get-tuple-element.52), calls=%async_computation.4 | async-start | bytes 262144 | tf_op jit(solution)/shard_map/all_to_all | solution.py:500
  110.2 0.0 copy-done.2
  110.2 0.0 copy-done.6
  110.2 0.0 copy-done.7
  110.2 0.0 copy-start.5
  110.2 1.4 %copy-done.5 = bf16[768,1024]{1,0:T(8,128)(2,1)S(1)} copy-done((bf16[768,1024]{1,0:T(8,128)(2,1)S(1)}, bf16[768,1024]{1,0:T(8,128)(2,1)}, u32[]{:S(2)}) %copy-start.5) | copy-done | bytes 1572888
  111.6 0.0 copy-start.3
  111.6 0.0 copy-start.4
  111.6 3.6 %shard_map.132 = bf16[4,192,1024]{2,1,0:T(8,128)(2,1)} custom-call(bf16[768,1024]{1,0:T(8,128)(2,1)S(1)} %copy-done.5, f32[768,16]{1,0:T(8,128)S(1)} %copy-done.6, bf16[1024,1024]{1,0:T(8,128)(2,1)S(1)} %copy-done.2, bf16[1024,48]{1,0:T(8,128)(2,1)S(1)} %copy-done.7), custom_call_target="tpu_custom_call" | custom-call | flops 2000000000 | bytes 6000000 | tf_op jit(solution)/shard_map/pallas_call | solution.py:484
  115.2 0.0 copy-done.3
  115.2 0.0 copy-done.4
  115.2 1.2 shard_map.136
  116.3 5.0 %all-to-all-done.4.got = bf16[16,8,512]{2,1,0:T(8,128)(2,1)S(1)} async-done(((bf16[16,8,512]{2,1,0:T(8,128)(2,1)}), bf16[16,8,512]{2,1,0:T(8,128)(2,1)S(1)}, u32[]{:S(2)}, u32[]{:S(2)}) %all-to-all-start.4) | async-done | bytes 131104 | tf_op jit(solution)/shard_map/all_to_all | solution.py:500
  121.3 0.7 shard_map.137
Async XLA Ops:
  0.6 0.8 copy-start.1
  2.2 29.0 %all-to-all-start = ((bf16[16,12,1024]{2,1,0:T(8,128)(2,1)}), bf16[16,12,1024]{2,1,0:T(8,128)(2,1)S(1)}, u32[]{:S(2)}, u32[]{:S(2)}) async-start(bf16[16,12,1024]{2,1,0:T(8,128)(2,1)} %shard_map.128), calls=%async_computation | async-start | bytes 1048576 | tf_op jit(solution)/shard_map/all_to_all | solution.py:389
  31.2 0.8 copy-start.8
  34.9 19.4 %all-to-all-start.1 = ((f32[16,48,128]{2,1,0:T(8,128)}), f32[16,48,128]{2,1,0:T(8,128)S(1)}, u32[]{:S(2)}, u32[]{:S(2)}) async-start(f32[16,48,128]{2,1,0:T(8,128)} %get-tuple-element.35), calls=%async_computation.1 | async-start | bytes 786432 | tf_op jit(solution)/shard_map/all_to_all | solution.py:429
  54.3 0.8 copy-start.9
  66.4 3.1 %collective-permute-start = (bf16[16,72,512]{2,1,0:T(8,128)(2,1)}, bf16[16,72,512]{2,1,0:T(8,128)(2,1)S(1)}, u32[]{:S(2)}, u32[]{:S(2)}) collective-permute-start(bf16[16,72,512]{2,1,0:T(8,128)(2,1)} %get-tuple-element.49), channel_id=1, source_target_pairs={{0,1},{1,0},{2,3},{3,2},{4,5},{5,4},{6,7},{7,6},{8,9},{9,8},{10,11... | collective-permute-start | bytes 3538952 | tf_op jit(solution)/shard_map/ppermute | solution.py:464
  69.5 1.3 %copy-start = (bf16[16,72,512]{2,1,0:T(8,128)(2,1)S(1)}, bf16[16,72,512]{2,1,0:T(8,128)(2,1)}, u32[]{:S(2)}) copy-start(bf16[16,72,512]{2,1,0:T(8,128)(2,1)} %get-tuple-element.48.keep) | copy-start | bytes 3538948
  71.1 39.0 %copy-start.2 = (bf16[1024,1024]{1,0:T(8,128)(2,1)S(1)}, bf16[1024,1024]{1,0:T(8,128)(2,1)}, u32[]{:S(2)}) copy-start(bf16[1024,1024]{1,0:T(8,128)(2,1)} %w_value.3) | copy-start | bytes 6291460
  94.1 16.1 %copy-start.6 = (f32[768,16]{1,0:T(8,128)S(1)}, f32[768,16]{1,0:T(8,128)}, u32[]{:S(2)}) copy-start(f32[768,16]{1,0:T(8,128)} %get-tuple-element.46.score_grad) | copy-start | bytes 147460
  94.1 16.1 %copy-start.7 = (bf16[1024,48]{1,0:T(8,128)(2,1)S(1)}, bf16[1024,48]{1,0:T(8,128)(2,1)}, u32[]{:S(2)}) copy-start(bf16[1024,48]{1,0:T(8,128)(2,1)} %get-tuple-element.47.fold_one) | copy-start | bytes 294916
  106.6 14.7 %all-to-all-start.4 = ((bf16[16,8,512]{2,1,0:T(8,128)(2,1)}), bf16[16,8,512]{2,1,0:T(8,128)(2,1)S(1)}, u32[]{:S(2)}, u32[]{:S(2)}) async-start(bf16[16,8,512]{2,1,0:T(8,128)(2,1)} %get-tuple-element.52), calls=%async_computation.4 | async-start | bytes 262144 | tf_op jit(solution)/shard_map/all_to_all | solution.py:500
  110.2 1.4 %copy-start.5 = (bf16[768,1024]{1,0:T(8,128)(2,1)S(1)}, bf16[768,1024]{1,0:T(8,128)(2,1)}, u32[]{:S(2)}) copy-start(bf16[768,1024]{1,0:T(8,128)(2,1)} %get-tuple-element.45.value_grad) | copy-start | bytes 4718596
  111.6 3.6 %copy-start.3 = (f32[1024]{0:T(1024)S(1)}, f32[1024]{0:T(1024)}, u32[]{:S(2)}) copy-start(f32[1024]{0:T(1024)} %param.12) | copy-start | bytes 12292
  111.6 3.6 %copy-start.4 = (f32[1024]{0:T(1024)S(1)}, f32[1024]{0:T(1024)}, u32[]{:S(2)}) copy-start(f32[1024]{0:T(1024)} %param.14) | copy-start | bytes 12292

commit v3 on v2

--- a/solution.py
+++ b/solution.py
@@ -86,18 +86,30 @@
 
 def forward_kernel(
     table, tok, w_value, w_key, w_key_two, query_one, query_two,
-    values, weights, agg, agg_t, tok_t, scores_two, fold_one, fold_two,
+    values, weights, agg, agg_t, tok_t, scores_two, fold_one, fold_two, cross,
+    wide,
 ):
     @pl.when(pl.program_id(0) == 0)
     def _():
         fold_one[...] = fold(w_key[...], query_one[...])
         fold_two[...] = fold(w_key_two[...], query_two[...])
+        row = lax.broadcasted_iota(jnp.int32, (HEADS, PAIRS), 0)
+        col = lax.broadcasted_iota(jnp.int32, (HEADS, PAIRS), 1)
+        copies = jnp.where(row == (col & (HEADS - 1)), 1.0, 0.0).astype(BF16)
+        own = (lax.broadcasted_iota(jnp.int32, (D, PAIRS), 0) >> SHIFT) == (
+            lax.broadcasted_iota(jnp.int32, (D, PAIRS), 1) >> 4
+        )
+        for k in range(2):
+            spot = nn(fold_two[:, k * HEADS : (k + 1) * HEADS], copies)
+            wide[k] = jnp.where(own, spot, 0.0).astype(BF16)
 
     flat = tok[...].reshape(TOK, D)
     tok_t[...] = flat.T
     scores = folded_dot(flat, fold_one[...])
     vals = nn(flat, w_value[...])
     values[...] = vals
+    high, low = split2(vals)
+    cross[...] = nn(high, wide[0]) + nn(high, wide[1]) + nn(low, wide[0])
     group = [table[c] for c in range(CH)]
     score = [scores[c * BLK : (c + 1) * BLK] for c in range(CH)]
     top = [
@@ -135,20 +147,17 @@
         out[k] = cot[0]
 
 
-def stats_kernel(agg, got, scores_two, dw_two, stats, cot, rows_f):
+def stats_kernel(agg, cot, scores_two, pair_two, stats):
     heads = spread(1)
-    for k in range(16):
-        rows_f[12 * k : 12 * k + 12] = got[k].astype(F32)
-    cot[...] = rows_f[...].astype(BF16)
     score, grad = [[], []], [[], []]
     for b in range(NB):
-        cot_f = rows_f[b * BLK : (b + 1) * BLK]
+        cot_f = cot[b * BLK : (b + 1) * BLK].astype(F32)
         for g in range(GR):
             rows = slice(b * AGG + g * BLK, b * AGG + (g + 1) * BLK)
             dw = head_sum(agg[rows].astype(F32) * cot_f, heads)
-            dw_two[rows] = dw
             grad[g].append(dw)
             score[g].append(scores_two[rows])
+            pair_two[rows] = jnp.concatenate([score[g][-1], dw], 1)
     score = [jnp.concatenate(s, 0) for s in score]
     grad = [jnp.concatenate(s, 0) for s in grad]
     top = jnp.maximum(score[0], score[1])
@@ -161,40 +170,33 @@
         stats[k] = both
 
 
-def pre_kernel(values, cot, fold_two, direct, cross):
+def pre_kernel(values, cot, weights, direct):
     heads = spread(1)
-    row = lax.broadcasted_iota(jnp.int32, (HEADS, PAIRS), 0)
-    col = lax.broadcasted_iota(jnp.int32, (HEADS, PAIRS), 1)
-    copies = jnp.where(row == (col & (HEADS - 1)), 1.0, 0.0).astype(BF16)
-    own = (lax.broadcasted_iota(jnp.int32, (D, PAIRS), 0) >> SHIFT) == (
-        lax.broadcasted_iota(jnp.int32, (D, PAIRS), 1) >> 4
-    )
-    wide = [
-        jnp.where(own, nn(fold_two[:, k * HEADS : (k + 1) * HEADS], copies), 0.0).astype(BF16)
-        for k in range(2)
-    ]
     for b in range(NB):
         trows = slice(b * TOK, (b + 1) * TOK)
         cot_f = cot[b * BLK : (b + 1) * BLK].astype(F32)
-        vals = values[trows]
-        direct[trows] = head_sum(jnp.concatenate([cot_f] * CH, 0) * vals, heads)
-        high, low = split2(vals)
-        cross[trows] = nn(high, wide[0]) + nn(high, wide[1]) + nn(low, wide[0])
+        direct[trows] = jnp.concatenate(
+            [weights[trows], head_sum(jnp.concatenate([cot_f] * CH, 0) * values[trows], heads)], 1
+        )
+
+
+def total_kernel(stats, out):
+    logs = stats[:, :24, :]
+    top = jnp.max(logs, 0)
+    expo = jnp.exp(logs - top[None])
+    total = jnp.sum(expo, 0)
+    out[:24] = top + jnp.log(total)
+    out[24:] = jnp.sum(expo * stats[:, 24:, :], 0) / total
 
 
 def back_kernel(
-    table, core, stats, cot_h, scores_h, dw_h, weights_h, fold_h, direct_h, cross_h, tok_h, agg_h,
-    key_h, key_two_h,
-    value_grad, score_grad_h, send_h, keep_h,
-    cot, scores_two, dw_two, weights, fold_two, direct, cross, tok_t, agg_t, w_key, w_key_two,
-    grad, sums, send, keep, score_grad, sems,
+    table, core, totals, cot_h, pair_h, weights_h, fold_h, tok_h, cross_h, agg_h, key_h, key_two_h,
+    value_grad, score_grad_h, send_h, extra,
+    cot, pair_two, weights, fold_two, tok_t, cross, agg_t, w_key, w_key_two,
+    grad, send, score_grad, sems,
 ):
-    sources = (
-        cot_h, scores_h, dw_h, weights_h, fold_h, tok_h, direct_h, cross_h, agg_h, key_h, key_two_h,
-    )
-    targets = (
-        cot, scores_two, dw_two, weights, fold_two, tok_t, direct, cross, agg_t, w_key, w_key_two,
-    )
+    sources = (cot_h, pair_h, weights_h, fold_h, tok_h, cross_h, agg_h, key_h, key_two_h)
+    targets = (cot, pair_two, weights, fold_two, tok_t, cross, agg_t, w_key, w_key_two)
     copies = [
         pltpu.make_async_copy(x, y, sems.at[k]) for k, (x, y) in enumerate(zip(sources, targets))
     ]
@@ -208,13 +210,8 @@
             [jnp.where(group[c] == 0, x[:BLK], x[BLK:]) for c in range(CH)], 0
         )
 
-    logs = stats[:, :24, :]
-    top = jnp.max(logs, 0)
-    expo = jnp.exp(logs - top[None])
-    total = jnp.sum(expo, 0)
-    inner = unpack(jnp.sum(expo * stats[:, 24:, :], 0) / total)
-    log_total = unpack(top + jnp.log(total))
-    for c in copies[:5]:
+    log_total, inner = unpack(totals[:24]), unpack(totals[24:])
+    for c in copies[:4]:
         c.wait()
     for c in copies[5:]:
         c.start()
@@ -224,32 +221,28 @@
         arows = slice(b * AGG, (b + 1) * AGG)
         trows = slice(b * TOK, (b + 1) * TOK)
         twice = lambda x: jnp.concatenate([x, x], 0)
-        w_now = jnp.exp(scores_two[arows] - twice(log_total[rows]))
-        s_now = w_now * (dw_two[arows] - twice(inner[rows]))
+        w_now = jnp.exp(pair_two[arows, :HEADS] - twice(log_total[rows]))
+        s_now = w_now * (pair_two[arows, HEADS:] - twice(inner[rows]))
         w_two.append(w_now)
         s_two.append(s_now)
         cot_f = cot[rows].astype(F32)
         agg_grad = expand(w_now, heads2) * twice(cot_f) + folded_back(s_now, fold_two[...])
-        grad[trows] = (expand(weights[trows], heads2) * by_channel(agg_grad)).astype(BF16)
+        weight = weights[trows, :HEADS]
+        grad[trows] = (expand(weight, heads2) * by_channel(agg_grad)).astype(BF16)
+    copies[4].wait()
     copies[5].wait()
-    for n in range(4):
-        cols = slice(n * 256, (n + 1) * 256)
-        out = nn(tok_t[...], grad[:, cols])
-        for p in range(16):
-            sums[p * SLAB : p * SLAB + 64, cols] = out[p * 64 : (p + 1) * 64]
     row = lax.broadcasted_iota(jnp.int32, (2 * HEADS, PAIRS), 0) & (HEADS - 1)
     col = lax.broadcasted_iota(jnp.int32, (2 * HEADS, PAIRS), 1)
     tiled = jnp.where(row == (col & (HEADS - 1)), 1.0, 0.0).astype(BF16)
     gather = jnp.where(row == (col >> 4), 1.0, 0.0).astype(BF16)[:HEADS]
-    copies[6].wait()
-    copies[7].wait()
     for b in range(NB):
         trows = slice(b * TOK, (b + 1) * TOK)
         score = by_channel(s_two[b])
         product = nn(jnp.concatenate(split2(score), 1), tiled) * cross[trows]
         high, low = split2(product)
-        dw = by_channel(w_two[b]) * direct[trows] + nt(high, gather) + nt(low, gather)
-        weight = weights[trows]
+        direct = weights[trows, HEADS:]
+        dw = by_channel(w_two[b]) * direct + nt(high, gather) + nt(low, gather)
+        weight = weights[trows, :HEADS]
         wdw = weight * dw
         part = [wdw[c * BLK : (c + 1) * BLK] for c in range(CH)]
         own = jnp.concatenate(
@@ -261,19 +254,19 @@
         both = nn(left, jnp.concatenate(split2(right), 1))
         return both[:, :HEADS] + both[:, HEADS:]
 
+    ones = outer(tok_t[...], score_grad[...])
+    copies[6].wait()
+    twos = outer(agg_t[...], jnp.concatenate(s_two, 0))
+    grads = jnp.concatenate([ones, twos, jnp.zeros((D, 128 - 2 * HEADS), F32)], 1).T[: 2 * HEADS]
+    copies[7].wait()
+    copies[8].wait()
     started = [
-        pltpu.make_async_copy(grad, value_grad, sems.at[11]),
-        pltpu.make_async_copy(score_grad, score_grad_h, sems.at[14]),
+        pltpu.make_async_copy(grad, value_grad, sems.at[9]),
+        pltpu.make_async_copy(score_grad, score_grad_h, sems.at[10]),
     ]
     for c in started:
         c.start()
-    ones = outer(tok_t[...], score_grad[...])
-    copies[8].wait()
-    twos = outer(agg_t[...], jnp.concatenate(s_two, 0))
-    grads = jnp.concatenate([ones, twos, jnp.zeros((D, 128 - 2 * HEADS), F32)], 1).T[: 2 * HEADS]
     lines = []
-    copies[9].wait()
-    copies[10].wait()
     for k, weight in enumerate((w_key, w_key_two)):
         high, low = split2(grads[k * HEADS : (k + 1) * HEADS])
         out = nn(jnp.concatenate([high, low], 0), weight[...])
@@ -283,38 +276,51 @@
         [line[:, k * 256 : (k + 1) * 256] for line in lines for k in range(4)], 0
     )
     left = (lax.broadcasted_iota(jnp.int32, (8, D), 1) & 64) == 0
-    pairs = []
-    for odd in range(2):
-        for k in range(2):
-            one, two = grads[16 * k : 16 * k + 8], grads[16 * k + 8 : 16 * k + 16]
-            if odd:
-                one = jnp.concatenate([one[:, 64:], one[:, :64]], 1)
-            else:
-                two = jnp.concatenate([two[:, D - 64 :], two[:, : D - 64]], 1)
-            pairs.append(jnp.where(left, one, two))
-    for p in range(16):
-        rows = slice(p * SLAB + 64, (p + 1) * SLAB)
-        lanes = slice((p // 2) * 128, (p // 2 + 1) * 128)
-        for half in (0, 512):
-            for k in range(2):
-                spot = slice(half + k * 128, half + (k + 1) * 128)
-                sums[rows, spot] = pairs[2 * (p % 2) + k][:, lanes]
-            sums[rows, half + 256 : half + 512] = quarters
+    even, odd = [], []
+    for k in range(2):
+        one, two = grads[16 * k : 16 * k + 8], grads[16 * k + 8 : 16 * k + 16]
+        even.append(jnp.where(left, one, jnp.concatenate([two[:, D - 64 :], two[:, : D - 64]], 1)))
+        odd.append(jnp.where(left, jnp.concatenate([one[:, 64:], one[:, :64]], 1), two))
     mine = core[0]
-    for which, (held, target) in enumerate(((send, send_h), (keep, keep_h))):
-        side = mine if which else 1 - mine
-        for k in range(8):
-            slab = sums[pl.ds(pl.multiple_of((2 * k + side) * SLAB, 8), SLAB), :]
+    here = [jnp.where(mine == 0, x, y) for x, y in zip(even, odd)]
+    away = [jnp.where(mine == 0, y, x) for x, y in zip(even, odd)]
+
+    def small(pair, k):
+        lanes = slice(k * 128, (k + 1) * 128)
+        return jnp.concatenate([pair[0][:, lanes], pair[1][:, lanes], quarters], 1)
+
+    for k in range(0, 8, 4):
+        out = nn(peer_rows(tok_t, k, 1 - mine), grad[...])
+        for i in range(4):
+            extra[k + i] = small(here, k + i)
+            other = small(away, k + i)
             for half in range(2):
-                held[8 * half + k] = slab[:, half * 512 : (half + 1) * 512].astype(held.dtype)
-        started.append(pltpu.make_async_copy(held, target, sems.at[12 + which]))
-        started[-1].start()
+                part = out[64 * i : 64 * (i + 1), half * 512 : (half + 1) * 512]
+                send[8 * half + k + i] = jnp.concatenate([part, other], 0).astype(BF16)
+    started.append(pltpu.make_async_copy(send, send_h, sems.at[11]))
+    started[-1].start()
     for c in started:
         c.wait()
 
 
+def peer_rows(tok_t, k, side):
+    return jnp.concatenate(
+        [tok_t[pl.ds(pl.multiple_of((2 * (k + i) + side) * 64, 64), 64), :] for i in range(4)], 0
+    )
+
+
+def keep_kernel(core, tok_t, value_grad, extra, keep):
+    mine = core[0]
+    for k in range(0, 8, 4):
+        out = nn(peer_rows(tok_t, k, mine), value_grad[...])
+        for i in range(4):
+            for half in range(2):
+                part = out[64 * i : 64 * (i + 1), half * 512 : (half + 1) * 512]
+                keep[8 * half + k + i] = jnp.concatenate([part, extra[k + i]], 0)
+
+
 def pair_kernel(keep, got, out):
-    out[...] = (keep[...].astype(F32) + got[...].astype(F32)).astype(BF16)
+    out[...] = (keep[...] + got[...].astype(F32)).astype(BF16)
 
 
 def token_kernel(value_grad, score_grad, w_value, fold_one, out):
@@ -385,13 +391,20 @@
 
 def shards(tokens, table, w_key, w_value, query_one, w_key_two, query_two, cotangent):
     query_one, query_two = query_one.reshape(1, D), query_two.reshape(1, D)
-    tiled = call(tile_kernel, shape((16, ROWS // 16, D), BF16), 10**4, 10**6, 4)(cotangent)
-    cot = lax.all_to_all(tiled, "chan", 0, 0, tiled=True)
+    vmem = pl.BlockSpec(memory_space=pltpu.VMEM)
+    hbm = pl.BlockSpec(memory_space=pltpu.HBM)
+    tiled = call(
+        tile_kernel,
+        shape((16, ROWS // 16, D), BF16),
+        10**4,
+        10**6,
+    )(cotangent)
+    cot = lax.all_to_all(tiled, "chan", 0, 0, tiled=True).reshape(ROWS, D)
     full = whole((D, D))
     by_rows = lambda n, w: pl.BlockSpec((n, w), lambda i: (i, 0))
     by_cols = lambda n: pl.BlockSpec((D, n), lambda i: (0, i))
     token_spec = pl.BlockSpec((CH, BLK, D), lambda i: (0, i, 0))
-    values, weights, agg, agg_t, tok_t, scores_two, fold_one, fold_two = call(
+    values, weights, agg, agg_t, tok_t, scores_two, fold_one, fold_two, cross = call(
         forward_kernel,
         (
             shape((NB * TOK, D), F32),
@@ -402,6 +415,7 @@
             shape((NB * AGG, HEADS), F32),
             shape((D, 3 * HEADS), BF16),
             shape((D, 3 * HEADS), BF16),
+            shape((NB * TOK, PAIRS), F32),
         ),
         4 * 10**9,
         16 * 10**6,
@@ -416,52 +430,53 @@
             by_rows(AGG, HEADS),
             whole((D, 3 * HEADS)),
             whole((D, 3 * HEADS)),
+            by_rows(TOK, PAIRS),
         ),
+        scratch_shapes=[pltpu.VMEM((2, D, PAIRS), BF16)],
     )(table, tokens, w_value, w_key, w_key_two, query_one, query_two)
-    dw_two, stats, cot = call(
+    pair_two, stats = call(
         stats_kernel,
-        (shape((NB * AGG, HEADS), F32), shape((16, 48, 128), F32), shape((ROWS, D), BF16)),
+        (shape((NB * AGG, 2 * HEADS), F32), shape((16, 48, 128), F32)),
         10**9,
         2 * 10**6,
-        scratch_shapes=[pltpu.VMEM((ROWS, D), F32)],
     )(agg, cot, scores_two)
-    stats, fold_now = lax.optimization_barrier((stats, fold_two))
+    stats, values, weights = lax.optimization_barrier((stats, values, weights))
     stats = lax.all_to_all(stats, "chan", 0, 0, tiled=True)
     core = lax.rem(lax.axis_index("patch"), 2).astype(jnp.int32).reshape(1)
-    direct, cross = call(
-        pre_kernel,
-        (shape((NB * TOK, HEADS), F32), shape((NB * TOK, PAIRS), F32)),
-        10**9,
-        5 * 10**6,
-    )(values, cot, fold_now)
-    vmem = pl.BlockSpec(memory_space=pltpu.VMEM)
-    hbm = pl.BlockSpec(memory_space=pltpu.HBM)
-    fetched = (
-        cot, scores_two, dw_two, weights, fold_two, direct, cross, tok_t, agg_t, w_key, w_key_two,
-    )
-    value_grad, score_grad, send, keep = call(
+    weights = call(
+        pre_kernel, shape((NB * TOK, 2 * HEADS), F32), 10**9, 5 * 10**6
+    )(values, cot, weights)
+    totals = call(total_kernel, shape((48, 128), F32), 10**6, 10**6, 4)(stats)
+    fetched = (cot, pair_two, weights, fold_two, tok_t, cross, agg_t, w_key, w_key_two)
+    value_grad, score_grad, send, extra = call(
         back_kernel,
         (
             shape((NB * TOK, D), BF16),
             shape((NB * TOK, HEADS), F32),
             shape((16, SLAB, 512), BF16),
-            shape((16, SLAB, 512), BF16),
+            shape((8, 8, 512), F32),
         ),
         4 * 10**9,
         16 * 10**6,
         in_specs=[SMEM, SMEM, vmem] + [hbm] * len(fetched),
-        out_specs=(hbm, hbm, hbm, hbm),
+        out_specs=(hbm, hbm, hbm, vmem),
         scratch_shapes=[pltpu.VMEM(x.shape, x.dtype) for x in fetched]
         + [
             pltpu.VMEM((NB * TOK, D), BF16),
-            pltpu.VMEM((16 * SLAB, D), F32),
-            pltpu.VMEM((16, SLAB, 512), BF16),
             pltpu.VMEM((16, SLAB, 512), BF16),
             pltpu.VMEM((NB * TOK, HEADS), F32),
-            pltpu.SemaphoreType.DMA((15,)),
+            pltpu.SemaphoreType.DMA((12,)),
         ],
-    )(table, core, stats, *fetched)
+    )(table, core, totals, *fetched)
     got = lax.ppermute(send, "patch", [(i, i ^ 1) for i in range(16)])
+    keep = call(
+        keep_kernel,
+        shape((16, SLAB, 512), F32),
+        10**9,
+        5 * 10**6,
+        16,
+        in_specs=[SMEM, vmem, vmem, vmem],
+    )(core, tok_t, value_grad, extra)
     slabs = pl.BlockSpec((4, SLAB, 512), lambda i: (i, 0, 0))
     pairs = call(
         pair_kernel,

time: 123 us -> 120 us (0.976)
  waiting for transfers between devices: 26.5 us -> 23.4 us
    ppermute x1, waiting for transfers between devices: 3.05 us -> 0.01 us  [shards(): got = lax.ppermute(send, 'patch', [(i, i ^ 1) for i in range(16)])]
    pallas_call x1, Pallas kernels: 11.3 us -> 9.55 us  [shards(): call(back_kernel, (shape((NB * TOK, D), BF16), shape((NB * TOK, HEADS), F...]
    all_to_all x1, waiting for transfers between devices: 10.4 us -> 12 us  [shards(): stats = lax.all_to_all(stats, 'chan', 0, 0, tiled=True)]
    pallas_call x1, Pallas kernels: 10.5 us -> 12 us  [shards(): call(forward_kernel, (shape((NB * TOK, D), F32), shape((NB * TOK, HEADS),...]
    all_to_all x1, waiting for transfers between devices: 8.11 us -> 6.65 us  [shards(): cot = lax.all_to_all(tiled, 'chan', 0, 0, tiled=True).reshape(ROWS, D)]
    pallas_call x3 -> x5, Pallas kernels: 9.18 us -> 9.24 us  [the longest x1 3.84 us: shards(): call(pre_kernel, shape((NB * TOK, 2 * HEADS), F32), 10 ** 9, 5 * 10 ** 6)]
  transfers between devices with their start and end apart: 4 -> 4, of which waited for: 4 -> 3; matrix products, arithmetic and copies ran while one was open for 0% -> 0% of each run, Pallas kernels for 17% -> 18%
where the time goes in v3:
time: 120 us; the launch traced here: 119 us
  Pallas kernels  37.4 us (31%)
  blocking collectives  35 us (29%)
  waiting for transfers between devices  23.4 us (20%)
  starting transfers between devices  17.5 us (15%)
  local copies, waits for them, and re-layouts  5.36 us (4%)
    all_to_all x1, blocking collectives, shards(): lax.all_to_all(pairs, ('chan', 'patch'), 0, 0, tiled=True, axis_index_gro...  23.3 us
    pallas_call x1, Pallas kernels, shards(): call(forward_kernel, (shape((NB * TOK, D), F32), shape((NB * TOK, HEADS),...  12 us
    all_to_all x1, waiting for transfers between devices, shards(): stats = lax.all_to_all(stats, 'chan', 0, 0, tiled=True)  12 us
    all_to_all x1, blocking collectives, shards(): lax.all_to_all(rows, 'chan', 0, 0, tiled=True, axis_index_groups=same_half)  11.7 us
    all_to_all x1, starting transfers between devices, shards(): cot = lax.all_to_all(tiled, 'chan', 0, 0, tiled=True).reshape(ROWS, D)  10.3 us
    pallas_call x1, Pallas kernels, shards(): call(back_kernel, (shape((NB * TOK, D), BF16), shape((NB * TOK, HEADS), F...  9.55 us
    all_to_all x1, waiting for transfers between devices, shards(): cot = lax.all_to_all(tiled, 'chan', 0, 0, tiled=True).reshape(ROWS, D)  6.65 us
    all_to_all x1, waiting for transfers between devices, shards(): rows = lax.all_to_all(rows, 'chan', 0, 0, tiled=True)  4.75 us
  transfers between devices with their start and end apart: 4, of which 3 were waited for; matrix products, arithmetic and copies ran while one was open for 0% of the time, Pallas kernels for 18%

profile of v3, /device:TPU:8, one launch (start us, length us, event | category | flops | bytes accessed | tf_op | source)
XLA Modules:
  0.0 119.4 jit_solution(6060742945348533347)
XLA Ops:
  0.6 1.6 %shard_map.128 = bf16[16,12,1024]{2,1,0:T(8,128)(2,1)} custom-call(bf16[1,12,1024]{2,1,0:T(8,128)(2,1)} %cot.1), custom_call_target="tpu_custom_call" | custom-call | flops 10000 | bytes 1000000 | tf_op jit(solution)/shard_map/pallas_call | solution.py:396
  2.2 10.3 %all-to-all-start = ((bf16[16,12,1024]{2,1,0:T(8,128)(2,1)}), bf16[16,12,1024]{2,1,0:T(8,128)(2,1)S(1)}, u32[]{:S(2)}, u32[]{:S(2)}) async-start(bf16[16,12,1024]{2,1,0:T(8,128)(2,1)} %shard_map.128), calls=%async_computation | async-start | bytes 1048576 | tf_op jit(solution)/shard_map/all_to_all | solution.py:402
  12.5 12.0 %shard_map.127 = (f32[768,1024]{1,0:T(8,128)}, f32[768,16]{1,0:T(8,128)}, bf16[384,1024]{1,0:T(8,128)(2,1)}, bf16[1024,384]{1,0:T(8,128)(2,1)}, bf16[1024,768]{1...) custom-call(s32[4]{0:T(128)} %table.3, ...), custom_call_target="tpu_custom_call" | custom-call | flops 4000000000 | bytes 16000000 | tf_op jit(solution)/shard_map/pallas_call | solution.py:407
  24.5 6.6 %all-to-all-done = bf16[16,12,1024]{2,1,0:T(8,128)(2,1)S(1)} async-done(((bf16[16,12,1024]{2,1,0:T(8,128)(2,1)}), bf16[16,12,1024]{2,1,0:T(8,128)(2,1)S(1)}, u32[]{:S(2)}, u32[]{:S(2)}) %all-to-all-start) | async-done | bytes 393248 | tf_op jit(solution)/shard_map/all_to_all | solution.py:402
  31.2 0.8 reshape.33.cot.cot_h
  32.0 2.8 %shard_map.129 = (f32[384,32]{1,0:T(8,128)}, f32[16,48,128]{2,1,0:T(8,128)}) custom-call(bf16[384,1024]{1,0:T(8,128)(2,1)} %get-tuple-element.30.agg, bf16[192,1024]{1,0:T(8,128)(2,1)} %reshape.33.cot.cot_h, f32[384,16]{1,0:T(8,128)} %get-tuple-element.31.scores_two), custom_call_target="tpu_custom_call" | custom-call | flops 1000000000 | bytes 2000000 | tf_op jit(solution)/shard_map/pallas_call | solution.py:437
  34.8 3.6 %all-to-all-start.1 = ((f32[16,48,128]{2,1,0:T(8,128)}), f32[16,48,128]{2,1,0:T(8,128)S(1)}, u32[]{:S(2)}, u32[]{:S(2)}) async-start(f32[16,48,128]{2,1,0:T(8,128)} %get-tuple-element.35), calls=%async_computation.1 | async-start | bytes 786432 | tf_op jit(solution)/shard_map/all_to_all | solution.py:444
  38.4 3.8 %shard_map.131.weights_h = f32[768,32]{1,0:T(8,128)} custom-call(f32[768,1024]{1,0:T(8,128)} %get-tuple-element.37.values, bf16[192,1024]{1,0:T(8,128)(2,1)} %reshape.33.cot.cot_h, f32[768,16]{1,0:T(8,128)} %get-tuple-element.38.weights), custom_call_target="tpu_custom_call" | custom-call | flops 1000000000 | bytes 5000000 | tf_op jit(solution)/shard_map/pallas_call | solution.py:446
  42.2 12.0 %all-to-all-done.1.stats = f32[16,48,128]{2,1,0:T(8,128)S(1)} async-done(((f32[16,48,128]{2,1,0:T(8,128)}), f32[16,48,128]{2,1,0:T(8,128)S(1)}, u32[]{:S(2)}, u32[]{:S(2)}) %all-to-all-start.1) | async-done | bytes 393248 | tf_op jit(solution)/shard_map/all_to_all | solution.py:444
  54.2 0.1 shard_map.130.totals
  54.3 0.0 copy-start.4
  54.3 0.6 copy-done.4
  54.9 0.0 copy-start
  54.9 9.5 %shard_map.132 = (bf16[768,1024]{1,0:T(8,128)(2,1)}, f32[768,16]{1,0:T(8,128)}, bf16[16,72,512]{2,1,0:T(8,128)(2,1)}, f32[8,8,512]{2,1,0:T(8,128)}) custom-call(s32[4]{0:T(128)} %table.3, s32[1]{0:T(128)} %bitcast.core, f32[48,128]{1,0:T(8,128)} %copy-done.4, bf16[192,1024]{1,0:T(8,128)(2,1)} %reshape.33.cot.cot_h, f32[384,32]{1,0:T(8,128)} %get-tuple-element.36.pair_h, ...), custom_call_target="tpu_custom_call" | custom-call | flops 4000000000 | bytes 16000000 | tf_op jit(solution)/shard_map/pallas_call | solution.py:451
  64.4 0.1 collective-permute-start
  64.5 0.0 copy-done
  64.5 0.0 copy-start.1
  64.5 1.4 %copy-done.1 = bf16[768,1024]{1,0:T(8,128)(2,1)S(1)} copy-done((bf16[768,1024]{1,0:T(8,128)(2,1)S(1)}, bf16[768,1024]{1,0:T(8,128)(2,1)}, u32[]{:S(2)}) %copy-start.1) | copy-done | bytes 1572888
  65.9 0.0 copy-start.3
  65.9 0.9 copy-done.3
  66.8 1.0 shard_map.134.keep
  67.8 0.0 collective-permute-done.got
  67.8 0.3 shard_map.135
  68.1 0.0 copy-start.9
  68.1 23.3 %all_to_all.25.got = bf16[16,72,512]{2,1,0:T(8,128)(2,1)S(1)} all-to-all(bf16[16,72,512]{2,1,0:T(8,128)(2,1)S(1)} %shard_map.135), channel_id=1, replica_groups={{0,2,4,6,8,10,12,14,16,18,20,22,24,26,28,30},{1,3,5,7,9,11,13,15,17,19,..., dimensions={0} | all-to-all | bytes 2359296 | tf_op jit(solution)/shard_map/all_to_all | solution.py:496
  91.4 0.0 copy-start.2
  91.4 0.0 copy-start.8
  91.4 0.2 shard_map.136
  91.6 11.7 %all_to_all.26.got = bf16[8,8,1024]{2,1,0:T(8,128)(2,1)S(1)} all-to-all(bf16[8,8,1024]{2,1,0:T(8,128)(2,1)S(1)} %shard_map.136), channel_id=1, replica_groups={{0,32,64,96,128,160,192,224},{16,48,80,112,144,176,208,240},{1,33,65,97..., dimensions={0} | all-to-all | bytes 262144 | tf_op jit(solution)/shard_map/all_to_all | solution.py:511
  103.3 0.7 shard_map.137
  104.0 3.5 %all-to-all-start.4 = ((bf16[16,8,512]{2,1,0:T(8,128)(2,1)}), bf16[16,8,512]{2,1,0:T(8,128)(2,1)S(1)}, u32[]{:S(2)}, u32[]{:S(2)}) async-start(bf16[16,8,512]{2,1,0:T(8,128)(2,1)} %get-tuple-element.50), calls=%async_computation.4 | async-start | bytes 262144 | tf_op jit(solution)/shard_map/all_to_all | solution.py:515
  107.5 0.0 copy-done.9
  107.5 0.0 copy-done.2
  107.5 0.0 copy-done.8
  107.5 0.0 copy-start.5
  107.5 1.6 %copy-done.5 = bf16[1024,1024]{1,0:T(8,128)(2,1)S(1)} copy-done((bf16[1024,1024]{1,0:T(8,128)(2,1)S(1)}, bf16[1024,1024]{1,0:T(8,128)(2,1)}, u32[]{:S(2)}) %copy-start.5) | copy-done | bytes 2097176
  109.1 0.0 copy-start.6
  109.1 0.0 copy-start.7
  109.1 3.6 %shard_map.133 = bf16[4,192,1024]{2,1,0:T(8,128)(2,1)} custom-call(bf16[768,1024]{1,0:T(8,128)(2,1)S(1)} %copy-done.2, f32[768,16]{1,0:T(8,128)S(1)} %copy-done.8, bf16[1024,1024]{1,0:T(8,128)(2,1)S(1)} %copy-done.5, bf16[1024,48]{1,0:T(8,128)(2,1)S(1)} %copy-done.9), custom_call_target="tpu_custom_call" | custom-call | flops 2000000000 | bytes 6000000 | tf_op jit(solution)/shard_map/pallas_call | solution.py:499
  112.7 0.0 copy-done.6
  112.7 0.0 copy-done.7
  112.7 1.2 shard_map.138
  113.9 4.8 %all-to-all-done.4.got = bf16[16,8,512]{2,1,0:T(8,128)(2,1)S(1)} async-done(((bf16[16,8,512]{2,1,0:T(8,128)(2,1)}), bf16[16,8,512]{2,1,0:T(8,128)(2,1)S(1)}, u32[]{:S(2)}, u32[]{:S(2)}) %all-to-all-start.4) | async-done | bytes 131104 | tf_op jit(solution)/shard_map/all_to_all | solution.py:515
  118.6 0.7 shard_map.139
Async XLA Ops:
  2.2 29.0 %all-to-all-start = ((bf16[16,12,1024]{2,1,0:T(8,128)(2,1)}), bf16[16,12,1024]{2,1,0:T(8,128)(2,1)S(1)}, u32[]{:S(2)}, u32[]{:S(2)}) async-start(bf16[16,12,1024]{2,1,0:T(8,128)(2,1)} %shard_map.128), calls=%async_computation | async-start | bytes 1048576 | tf_op jit(solution)/shard_map/all_to_all | solution.py:402
  34.8 19.4 %all-to-all-start.1 = ((f32[16,48,128]{2,1,0:T(8,128)}), f32[16,48,128]{2,1,0:T(8,128)S(1)}, u32[]{:S(2)}, u32[]{:S(2)}) async-start(f32[16,48,128]{2,1,0:T(8,128)} %get-tuple-element.35), calls=%async_computation.1 | async-start | bytes 786432 | tf_op jit(solution)/shard_map/all_to_all | solution.py:444
  54.3 0.6 copy-start.4
  54.9 9.7 %copy-start = (bf16[1024,768]{1,0:T(8,128)(2,1)S(1)}, bf16[1024,768]{1,0:T(8,128)(2,1)}, u32[]{:S(2)}) copy-start(bf16[1024,768]{1,0:T(8,128)(2,1)} %get-tuple-element.40.tok_h.tok_t) | copy-start | bytes 4718596
  64.4 3.4 %collective-permute-start = (bf16[16,72,512]{2,1,0:T(8,128)(2,1)}, bf16[16,72,512]{2,1,0:T(8,128)(2,1)S(1)}, u32[]{:S(2)}, u32[]{:S(2)}) collective-permute-start(bf16[16,72,512]{2,1,0:T(8,128)(2,1)} %get-tuple-element.47), channel_id=1, source_target_pairs={{0,1},{1,0},{2,3},{3,2},{4,5},{5,4},{6,7},{7,6},{8,9},{9,8},{10,11... | collective-permute-start | bytes 3538952 | tf_op jit(solution)/shard_map/ppermute | solution.py:471
  64.5 1.4 %copy-start.1 = (bf16[768,1024]{1,0:T(8,128)(2,1)S(1)}, bf16[768,1024]{1,0:T(8,128)(2,1)}, u32[]{:S(2)}) copy-start(bf16[768,1024]{1,0:T(8,128)(2,1)} %get-tuple-element.43.value_grad) | copy-start | bytes 4718596
  65.9 0.9 copy-start.3
  68.1 39.4 %copy-start.9 = (bf16[1024,48]{1,0:T(8,128)(2,1)S(1)}, bf16[1024,48]{1,0:T(8,128)(2,1)}, u32[]{:S(2)}) copy-start(bf16[1024,48]{1,0:T(8,128)(2,1)} %get-tuple-element.45.fold_one) | copy-start | bytes 294916
  91.4 16.1 %copy-start.2 = (bf16[768,1024]{1,0:T(8,128)(2,1)S(1)}, bf16[768,1024]{1,0:T(8,128)(2,1)}, u32[]{:S(2)}) copy-start(bf16[768,1024]{1,0:T(8,128)(2,1)} %get-tuple-element.43.value_grad) | copy-start | bytes 4718596
  91.4 16.1 %copy-start.8 = (f32[768,16]{1,0:T(8,128)S(1)}, f32[768,16]{1,0:T(8,128)}, u32[]{:S(2)}) copy-start(f32[768,16]{1,0:T(8,128)} %get-tuple-element.44.score_grad) | copy-start | bytes 147460
  104.0 14.7 %all-to-all-start.4 = ((bf16[16,8,512]{2,1,0:T(8,128)(2,1)}), bf16[16,8,512]{2,1,0:T(8,128)(2,1)S(1)}, u32[]{:S(2)}, u32[]{:S(2)}) async-start(bf16[16,8,512]{2,1,0:T(8,128)(2,1)} %get-tuple-element.50), calls=%async_computation.4 | async-start | bytes 262144 | tf_op jit(solution)/shard_map/all_to_all | solution.py:515
  107.5 1.6 %copy-start.5 = (bf16[1024,1024]{1,0:T(8,128)(2,1)S(1)}, bf16[1024,1024]{1,0:T(8,128)(2,1)}, u32[]{:S(2)}) copy-start(bf16[1024,1024]{1,0:T(8,128)(2,1)} %w_value.3) | copy-start | bytes 6291460
  109.1 3.6 %copy-start.6 = (f32[1024]{0:T(1024)S(1)}, f32[1024]{0:T(1024)}, u32[]{:S(2)}) copy-start(f32[1024]{0:T(1024)} %param.12) | copy-start | bytes 12292
  109.1 3.6 %copy-start.7 = (f32[1024]{0:T(1024)S(1)}, f32[1024]{0:T(1024)}, u32[]{:S(2)}) copy-start(f32[1024]{0:T(1024)} %param.14) | copy-start | bytes 12292

commit v4 on v3

--- a/solution.py
+++ b/solution.py
@@ -190,16 +190,18 @@
 
 
 def back_kernel(
-    table, core, totals, cot_h, pair_h, weights_h, fold_h, tok_h, cross_h, agg_h, key_h, key_two_h,
-    value_grad, score_grad_h, send_h, extra,
-    cot, pair_two, weights, fold_two, tok_t, cross, agg_t, w_key, w_key_two,
-    grad, send, score_grad, sems,
+    table, core, totals_h, cot_h, pair_h, weights_h, fold_h, tok_h, cross_h, agg_h, key_h, key_two_h,
+    value_grad, score_grad_h, send_h, extra_h,
+    totals, cot, pair_two, weights, fold_two, tok_t, cross, agg_t, w_key, w_key_two,
+    grad, send, score_grad, extra, sems,
 ):
     sources = (cot_h, pair_h, weights_h, fold_h, tok_h, cross_h, agg_h, key_h, key_two_h)
     targets = (cot, pair_two, weights, fold_two, tok_t, cross, agg_t, w_key, w_key_two)
     copies = [
         pltpu.make_async_copy(x, y, sems.at[k]) for k, (x, y) in enumerate(zip(sources, targets))
     ]
+    first = pltpu.make_async_copy(totals_h, totals, sems.at[12])
+    first.start()
     for c in copies[:5]:
         c.start()
     heads, heads2 = spread(1), spread(2)
@@ -210,6 +212,7 @@
             [jnp.where(group[c] == 0, x[:BLK], x[BLK:]) for c in range(CH)], 0
         )
 
+    first.wait()
     log_total, inner = unpack(totals[:24]), unpack(totals[24:])
     for c in copies[:4]:
         c.wait()
@@ -229,6 +232,8 @@
         agg_grad = expand(w_now, heads2) * twice(cot_f) + folded_back(s_now, fold_two[...])
         weight = weights[trows, :HEADS]
         grad[trows] = (expand(weight, heads2) * by_channel(agg_grad)).astype(BF16)
+    started = [pltpu.make_async_copy(grad, value_grad, sems.at[9])]
+    started[0].start()
     copies[4].wait()
     copies[5].wait()
     row = lax.broadcasted_iota(jnp.int32, (2 * HEADS, PAIRS), 0) & (HEADS - 1)
@@ -251,21 +256,18 @@
         score_grad[trows] = weight * (dw - by_channel(own))
 
     def outer(left, right):
-        both = nn(left, jnp.concatenate(split2(right), 1))
-        return both[:, :HEADS] + both[:, HEADS:]
+        right = jnp.concatenate([right, jnp.zeros((right.shape[0], 128 - HEADS), F32)], 1).T
+        both = nt(jnp.concatenate(split2(right[:HEADS]), 0), left)
+        return both[:HEADS] + both[HEADS:]
 
     ones = outer(tok_t[...], score_grad[...])
     copies[6].wait()
     twos = outer(agg_t[...], jnp.concatenate(s_two, 0))
-    grads = jnp.concatenate([ones, twos, jnp.zeros((D, 128 - 2 * HEADS), F32)], 1).T[: 2 * HEADS]
+    grads = jnp.concatenate([ones, twos], 0)
     copies[7].wait()
     copies[8].wait()
-    started = [
-        pltpu.make_async_copy(grad, value_grad, sems.at[9]),
-        pltpu.make_async_copy(score_grad, score_grad_h, sems.at[10]),
-    ]
-    for c in started:
-        c.start()
+    started.append(pltpu.make_async_copy(score_grad, score_grad_h, sems.at[10]))
+    started[-1].start()
     lines = []
     for k, weight in enumerate((w_key, w_key_two)):
         high, low = split2(grads[k * HEADS : (k + 1) * HEADS])
@@ -298,7 +300,9 @@
                 part = out[64 * i : 64 * (i + 1), half * 512 : (half + 1) * 512]
                 send[8 * half + k + i] = jnp.concatenate([part, other], 0).astype(BF16)
     started.append(pltpu.make_async_copy(send, send_h, sems.at[11]))
-    started[-1].start()
+    started.append(pltpu.make_async_copy(extra, extra_h, sems.at[13]))
+    for c in started[-2:]:
+        c.start()
     for c in started:
         c.wait()
 
@@ -383,7 +387,7 @@
     return pl.pallas_call(
         kernel,
         out_shape=out_shape,
-        compiler_params=pltpu.CompilerParams(vmem_limit_bytes=limit * MIB),
+        compiler_params=pltpu.CompilerParams(vmem_limit_bytes=int(limit * MIB)),
         cost_estimate=pl.CostEstimate(flops=flops, bytes_accessed=nbytes, transcendentals=0),
         **kw,
     )
@@ -458,14 +462,16 @@
         ),
         4 * 10**9,
         16 * 10**6,
-        in_specs=[SMEM, SMEM, vmem] + [hbm] * len(fetched),
-        out_specs=(hbm, hbm, hbm, vmem),
-        scratch_shapes=[pltpu.VMEM(x.shape, x.dtype) for x in fetched]
+        53.7,
+        in_specs=[SMEM, SMEM] + [hbm] * (1 + len(fetched)),
+        out_specs=(hbm, hbm, hbm, hbm),
+        scratch_shapes=[pltpu.VMEM(x.shape, x.dtype) for x in (totals,) + fetched]
         + [
             pltpu.VMEM((NB * TOK, D), BF16),
             pltpu.VMEM((16, SLAB, 512), BF16),
             pltpu.VMEM((NB * TOK, HEADS), F32),
-            pltpu.SemaphoreType.DMA((12,)),
+            pltpu.VMEM((8, 8, 512), F32),
+            pltpu.SemaphoreType.DMA((14,)),
         ],
     )(table, core, totals, *fetched)
     got = lax.ppermute(send, "patch", [(i, i ^ 1) for i in range(16)])

time: 120 us -> 117 us (0.975)
  Pallas kernels: 37.4 us -> 35.9 us
  local copies, waits for them, and re-layouts: 5.36 us -> 3.87 us
    unnamed x20 -> x18, local copies, waits for them, and re-layouts: 4.51 us -> 3.02 us
    pallas_call x1, Pallas kernels: 9.55 us -> 8.06 us  [shards(): call(back_kernel, (shape((NB * TOK, D), BF16), shape((NB * TOK, HEADS), F...]
  transfers between devices with their start and end apart: 4 -> 4, of which waited for: 3 -> 4; matrix products, arithmetic and copies ran while one was open for 0% -> 0% of each run, Pallas kernels for 18% -> 19%
where the time goes in v4:
time: 117 us
  Pallas kernels  35.9 us (31%)
  blocking collectives  34.6 us (30%)
  waiting for transfers between devices  24 us (21%)
  starting transfers between devices  17.5 us (15%)
  local copies, waits for them, and re-layouts  3.87 us (3%)
    all_to_all x1, blocking collectives, shards(): lax.all_to_all(pairs, ('chan', 'patch'), 0, 0, tiled=True, axis_index_gro...  22.9 us
    pallas_call x1, Pallas kernels, shards(): call(forward_kernel, (shape((NB * TOK, D), F32), shape((NB * TOK, HEADS),...  12 us
    all_to_all x1, waiting for transfers between devices, shards(): stats = lax.all_to_all(stats, 'chan', 0, 0, tiled=True)  12 us
    all_to_all x1, blocking collectives, shards(): lax.all_to_all(rows, 'chan', 0, 0, tiled=True, axis_index_groups=same_half)  11.7 us
    all_to_all x1, starting transfers between devices, shards(): cot = lax.all_to_all(tiled, 'chan', 0, 0, tiled=True).reshape(ROWS, D)  10.3 us
    pallas_call x1, Pallas kernels, shards(): call(back_kernel, (shape((NB * TOK, D), BF16), shape((NB * TOK, HEADS), F...  8.06 us
    all_to_all x1, waiting for transfers between devices, shards(): cot = lax.all_to_all(tiled, 'chan', 0, 0, tiled=True).reshape(ROWS, D)  6.64 us
    all_to_all x1, waiting for transfers between devices, shards(): rows = lax.all_to_all(rows, 'chan', 0, 0, tiled=True)  4.77 us
  transfers between devices with their start and end apart: 4, of which 4 were waited for; matrix products, arithmetic and copies ran while one was open for 0% of the time, Pallas kernels for 19%

profile of v4, /device:TPU:8, one launch (start us, length us, event | category | flops | bytes accessed | tf_op | source)
XLA Modules:
  0.0 116.7 jit_solution(14846401846956642541)
XLA Ops:
  0.6 1.6 %shard_map.128 = bf16[16,12,1024]{2,1,0:T(8,128)(2,1)} custom-call(bf16[1,12,1024]{2,1,0:T(8,128)(2,1)} %cot.1), custom_call_target="tpu_custom_call" | custom-call | flops 10000 | bytes 1000000 | tf_op jit(solution)/shard_map/pallas_call | solution.py:400
  2.2 10.3 %all-to-all-start = ((bf16[16,12,1024]{2,1,0:T(8,128)(2,1)}), bf16[16,12,1024]{2,1,0:T(8,128)(2,1)S(1)}, u32[]{:S(2)}, u32[]{:S(2)}) async-start(bf16[16,12,1024]{2,1,0:T(8,128)(2,1)} %shard_map.128), calls=%async_computation | async-start | bytes 1048576 | tf_op jit(solution)/shard_map/all_to_all | solution.py:406
  12.5 12.0 %shard_map.127 = (f32[768,1024]{1,0:T(8,128)}, f32[768,16]{1,0:T(8,128)}, bf16[384,1024]{1,0:T(8,128)(2,1)}, bf16[1024,384]{1,0:T(8,128)(2,1)}, bf16[1024,768]{1...) custom-call(s32[4]{0:T(128)} %table.3, ...), custom_call_target="tpu_custom_call" | custom-call | flops 4000000000 | bytes 16000000 | tf_op jit(solution)/shard_map/pallas_call | solution.py:411
  24.6 6.6 %all-to-all-done = bf16[16,12,1024]{2,1,0:T(8,128)(2,1)S(1)} async-done(((bf16[16,12,1024]{2,1,0:T(8,128)(2,1)}), bf16[16,12,1024]{2,1,0:T(8,128)(2,1)S(1)}, u32[]{:S(2)}, u32[]{:S(2)}) %all-to-all-start) | async-done | bytes 393248 | tf_op jit(solution)/shard_map/all_to_all | solution.py:406
  31.2 0.8 reshape.33.cot.cot_h
  32.0 2.8 %shard_map.129 = (f32[384,32]{1,0:T(8,128)}, f32[16,48,128]{2,1,0:T(8,128)}) custom-call(bf16[384,1024]{1,0:T(8,128)(2,1)} %get-tuple-element.30.agg, bf16[192,1024]{1,0:T(8,128)(2,1)} %reshape.33.cot.cot_h, f32[384,16]{1,0:T(8,128)} %get-tuple-element.31.scores_two), custom_call_target="tpu_custom_call" | custom-call | flops 1000000000 | bytes 2000000 | tf_op jit(solution)/shard_map/pallas_call | solution.py:441
  34.8 3.6 %all-to-all-start.1 = ((f32[16,48,128]{2,1,0:T(8,128)}), f32[16,48,128]{2,1,0:T(8,128)S(1)}, u32[]{:S(2)}, u32[]{:S(2)}) async-start(f32[16,48,128]{2,1,0:T(8,128)} %get-tuple-element.35), calls=%async_computation.1 | async-start | bytes 786432 | tf_op jit(solution)/shard_map/all_to_all | solution.py:448
  38.4 0.0 copy-start.6
  38.4 3.8 %shard_map.131.weights_h = f32[768,32]{1,0:T(8,128)} custom-call(f32[768,1024]{1,0:T(8,128)} %get-tuple-element.37.values, bf16[192,1024]{1,0:T(8,128)(2,1)} %reshape.33.cot.cot_h, f32[768,16]{1,0:T(8,128)} %get-tuple-element.38.weights), custom_call_target="tpu_custom_call" | custom-call | flops 1000000000 | bytes 5000000 | tf_op jit(solution)/shard_map/pallas_call | solution.py:450
  42.3 12.0 %all-to-all-done.1.stats = f32[16,48,128]{2,1,0:T(8,128)S(1)} async-done(((f32[16,48,128]{2,1,0:T(8,128)}), f32[16,48,128]{2,1,0:T(8,128)S(1)}, u32[]{:S(2)}, u32[]{:S(2)}) %all-to-all-start.1) | async-done | bytes 393248 | tf_op jit(solution)/shard_map/all_to_all | solution.py:448
  54.2 0.1 shard_map.130.totals_h
  54.3 0.0 copy-done.6
  54.3 0.0 copy-start
  54.3 8.1 %shard_map.132 = (bf16[768,1024]{1,0:T(8,128)(2,1)}, f32[768,16]{1,0:T(8,128)}, bf16[16,72,512]{2,1,0:T(8,128)(2,1)}, f32[8,8,512]{2,1,0:T(8,128)S(1)}) custom-call(s32[4]{0:T(128)S(1)} %copy-done.6, s32[1]{0:T(128)} %bitcast.core, f32[48,128]{1,0:T(8,128)S(1)} %shard_map.130.totals_h, bf16[192,1024]{1,0:T(8,128)(2,1)} %reshape.33.cot.cot_h, ...), custom_call_target="tpu_custom_call" | custom-call | flops 4000000000 | bytes 16000000 | tf_op jit(solution)/shard_map/pallas_call | solution.py:455
  62.4 0.1 collective-permute-start
  62.5 0.0 copy-done
  62.5 0.0 copy-start.1
  62.5 1.4 %copy-done.1 = bf16[768,1024]{1,0:T(8,128)(2,1)S(1)} copy-done((bf16[768,1024]{1,0:T(8,128)(2,1)S(1)}, bf16[768,1024]{1,0:T(8,128)(2,1)}, u32[]{:S(2)}) %copy-start.1) | copy-done | bytes 1572888
  63.9 1.0 shard_map.134.keep
  64.9 0.6 collective-permute-done.got
  65.5 0.3 shard_map.135
  65.8 0.0 copy-start.8
  65.8 22.9 %all_to_all.25.got = bf16[16,72,512]{2,1,0:T(8,128)(2,1)S(1)} all-to-all(bf16[16,72,512]{2,1,0:T(8,128)(2,1)S(1)} %shard_map.135), channel_id=1, replica_groups={{0,2,4,6,8,10,12,14,16,18,20,22,24,26,28,30},{1,3,5,7,9,11,13,15,17,19,..., dimensions={0} | all-to-all | bytes 2359296 | tf_op jit(solution)/shard_map/all_to_all | solution.py:502
  88.7 0.0 copy-start.2
  88.7 0.0 copy-start.7
  88.7 0.2 shard_map.136
  88.9 11.7 %all_to_all.26.got = bf16[8,8,1024]{2,1,0:T(8,128)(2,1)S(1)} all-to-all(bf16[8,8,1024]{2,1,0:T(8,128)(2,1)S(1)} %shard_map.136), channel_id=1, replica_groups={{0,32,64,96,128,160,192,224},{16,48,80,112,144,176,208,240},{1,33,65,97..., dimensions={0} | all-to-all | bytes 262144 | tf_op jit(solution)/shard_map/all_to_all | solution.py:517
  100.6 0.7 shard_map.137
  101.3 3.5 %all-to-all-start.4 = ((bf16[16,8,512]{2,1,0:T(8,128)(2,1)}), bf16[16,8,512]{2,1,0:T(8,128)(2,1)S(1)}, u32[]{:S(2)}, u32[]{:S(2)}) async-start(bf16[16,8,512]{2,1,0:T(8,128)(2,1)} %get-tuple-element.50), calls=%async_computation.4 | async-start | bytes 262144 | tf_op jit(solution)/shard_map/all_to_all | solution.py:521
  104.8 0.0 copy-done.8
  104.8 0.0 copy-done.2
  104.8 0.0 copy-done.7
  104.8 0.0 copy-start.3
  104.8 1.6 %copy-done.3 = bf16[1024,1024]{1,0:T(8,128)(2,1)S(1)} copy-done((bf16[1024,1024]{1,0:T(8,128)(2,1)S(1)}, bf16[1024,1024]{1,0:T(8,128)(2,1)}, u32[]{:S(2)}) %copy-start.3) | copy-done | bytes 2097176
  106.4 0.0 copy-start.4
  106.4 0.0 copy-start.5
  106.4 3.6 %shard_map.133 = bf16[4,192,1024]{2,1,0:T(8,128)(2,1)} custom-call(bf16[768,1024]{1,0:T(8,128)(2,1)S(1)} %copy-done.2, f32[768,16]{1,0:T(8,128)S(1)} %copy-done.7, bf16[1024,1024]{1,0:T(8,128)(2,1)S(1)} %copy-done.3, bf16[1024,48]{1,0:T(8,128)(2,1)S(1)} %copy-done.8), custom_call_target="tpu_custom_call" | custom-call | flops 2000000000 | bytes 6000000 | tf_op jit(solution)/shard_map/pallas_call | solution.py:505
  110.0 0.0 copy-done.4
  110.0 0.0 copy-done.5
  110.0 1.2 shard_map.138
  111.2 4.8 %all-to-all-done.4.got = bf16[16,8,512]{2,1,0:T(8,128)(2,1)S(1)} async-done(((bf16[16,8,512]{2,1,0:T(8,128)(2,1)}), bf16[16,8,512]{2,1,0:T(8,128)(2,1)S(1)}, u32[]{:S(2)}, u32[]{:S(2)}) %all-to-all-start.4) | async-done | bytes 131104 | tf_op jit(solution)/shard_map/all_to_all | solution.py:521
  116.0 0.7 shard_map.139
Async XLA Ops:
  2.2 29.0 %all-to-all-start = ((bf16[16,12,1024]{2,1,0:T(8,128)(2,1)}), bf16[16,12,1024]{2,1,0:T(8,128)(2,1)S(1)}, u32[]{:S(2)}, u32[]{:S(2)}) async-start(bf16[16,12,1024]{2,1,0:T(8,128)(2,1)} %shard_map.128), calls=%async_computation | async-start | bytes 1048576 | tf_op jit(solution)/shard_map/all_to_all | solution.py:406
  34.8 19.4 %all-to-all-start.1 = ((f32[16,48,128]{2,1,0:T(8,128)}), f32[16,48,128]{2,1,0:T(8,128)S(1)}, u32[]{:S(2)}, u32[]{:S(2)}) async-start(f32[16,48,128]{2,1,0:T(8,128)} %get-tuple-element.35), calls=%async_computation.1 | async-start | bytes 786432 | tf_op jit(solution)/shard_map/all_to_all | solution.py:448
  38.4 15.9 %copy-start.6 = (s32[4]{0:T(128)S(1)}, s32[4]{0:T(128)}, u32[]{:S(2)}) copy-start(s32[4]{0:T(128)} %table.3) | copy-start | bytes 52
  54.3 8.2 %copy-start = (bf16[1024,768]{1,0:T(8,128)(2,1)S(1)}, bf16[1024,768]{1,0:T(8,128)(2,1)}, u32[]{:S(2)}) copy-start(bf16[1024,768]{1,0:T(8,128)(2,1)} %get-tuple-element.40.tok_h.tok_t) | copy-start | bytes 4718596
  62.4 3.1 %collective-permute-start = (bf16[16,72,512]{2,1,0:T(8,128)(2,1)}, bf16[16,72,512]{2,1,0:T(8,128)(2,1)S(1)}, u32[]{:S(2)}, u32[]{:S(2)}) collective-permute-start(bf16[16,72,512]{2,1,0:T(8,128)(2,1)} %get-tuple-element.47), channel_id=1, source_target_pairs={{0,1},{1,0},{2,3},{3,2},{4,5},{5,4},{6,7},{7,6},{8,9},{9,8},{10,11... | collective-permute-start | bytes 3538952 | tf_op jit(solution)/shard_map/ppermute | solution.py:477
  62.5 1.4 %copy-start.1 = (bf16[768,1024]{1,0:T(8,128)(2,1)S(1)}, bf16[768,1024]{1,0:T(8,128)(2,1)}, u32[]{:S(2)}) copy-start(bf16[768,1024]{1,0:T(8,128)(2,1)} %get-tuple-element.43.value_grad) | copy-start | bytes 4718596
  65.8 39.0 %copy-start.8 = (bf16[1024,48]{1,0:T(8,128)(2,1)S(1)}, bf16[1024,48]{1,0:T(8,128)(2,1)}, u32[]{:S(2)}) copy-start(bf16[1024,48]{1,0:T(8,128)(2,1)} %get-tuple-element.45.fold_one) | copy-start | bytes 294916
  88.7 16.1 %copy-start.2 = (bf16[768,1024]{1,0:T(8,128)(2,1)S(1)}, bf16[768,1024]{1,0:T(8,128)(2,1)}, u32[]{:S(2)}) copy-start(bf16[768,1024]{1,0:T(8,128)(2,1)} %get-tuple-element.43.value_grad) | copy-start | bytes 4718596
  88.7 16.1 %copy-start.7 = (f32[768,16]{1,0:T(8,128)S(1)}, f32[768,16]{1,0:T(8,128)}, u32[]{:S(2)}) copy-start(f32[768,16]{1,0:T(8,128)} %get-tuple-element.44.score_grad) | copy-start | bytes 147460
  101.3 14.7 %all-to-all-start.4 = ((bf16[16,8,512]{2,1,0:T(8,128)(2,1)}), bf16[16,8,512]{2,1,0:T(8,128)(2,1)S(1)}, u32[]{:S(2)}, u32[]{:S(2)}) async-start(bf16[16,8,512]{2,1,0:T(8,128)(2,1)} %get-tuple-element.50), calls=%async_computation.4 | async-start | bytes 262144 | tf_op jit(solution)/shard_map/all_to_all | solution.py:521
  104.8 1.6 %copy-start.3 = (bf16[1024,1024]{1,0:T(8,128)(2,1)S(1)}, bf16[1024,1024]{1,0:T(8,128)(2,1)}, u32[]{:S(2)}) copy-start(bf16[1024,1024]{1,0:T(8,128)(2,1)} %w_value.3) | copy-start | bytes 6291460
  106.4 3.6 %copy-start.4 = (f32[1024]{0:T(1024)S(1)}, f32[1024]{0:T(1024)}, u32[]{:S(2)}) copy-start(f32[1024]{0:T(1024)} %param.12) | copy-start | bytes 12292
  106.4 3.6 %copy-start.5 = (f32[1024]{0:T(1024)S(1)}, f32[1024]{0:T(1024)}, u32[]{:S(2)}) copy-start(f32[1024]{0:T(1024)} %param.14) | copy-start | bytes 12292

commit v5 on v4

--- a/solution.py
+++ b/solution.py
@@ -193,7 +193,7 @@
     table, core, totals_h, cot_h, pair_h, weights_h, fold_h, tok_h, cross_h, agg_h, key_h, key_two_h,
     value_grad, score_grad_h, send_h, extra_h,
     totals, cot, pair_two, weights, fold_two, tok_t, cross, agg_t, w_key, w_key_two,
-    grad, send, score_grad, extra, sems,
+    grad, send, score_grad, score_turned, extra, sems,
 ):
     sources = (cot_h, pair_h, weights_h, fold_h, tok_h, cross_h, agg_h, key_h, key_two_h)
     targets = (cot, pair_two, weights, fold_two, tok_t, cross, agg_t, w_key, w_key_two)
@@ -232,8 +232,6 @@
         agg_grad = expand(w_now, heads2) * twice(cot_f) + folded_back(s_now, fold_two[...])
         weight = weights[trows, :HEADS]
         grad[trows] = (expand(weight, heads2) * by_channel(agg_grad)).astype(BF16)
-    started = [pltpu.make_async_copy(grad, value_grad, sems.at[9])]
-    started[0].start()
     copies[4].wait()
     copies[5].wait()
     row = lax.broadcasted_iota(jnp.int32, (2 * HEADS, PAIRS), 0) & (HEADS - 1)
@@ -255,19 +253,26 @@
         )
         score_grad[trows] = weight * (dw - by_channel(own))
 
+    def turn(x):
+        return jnp.concatenate([x, jnp.zeros((x.shape[0], 128 - HEADS), F32)], 1).T[:HEADS]
+
     def outer(left, right):
-        right = jnp.concatenate([right, jnp.zeros((right.shape[0], 128 - HEADS), F32)], 1).T
-        both = nt(jnp.concatenate(split2(right[:HEADS]), 0), left)
+        both = nt(jnp.concatenate(split2(right), 0), left)
         return both[:HEADS] + both[HEADS:]
 
-    ones = outer(tok_t[...], score_grad[...])
+    score_turned[...] = turn(score_grad[...])
+    ones = outer(tok_t[...], score_turned[...])
     copies[6].wait()
-    twos = outer(agg_t[...], jnp.concatenate(s_two, 0))
+    twos = outer(agg_t[...], turn(jnp.concatenate(s_two, 0)))
     grads = jnp.concatenate([ones, twos], 0)
     copies[7].wait()
     copies[8].wait()
-    started.append(pltpu.make_async_copy(score_grad, score_grad_h, sems.at[10]))
-    started[-1].start()
+    started = [
+        pltpu.make_async_copy(grad, value_grad, sems.at[9]),
+        pltpu.make_async_copy(score_turned, score_grad_h, sems.at[10]),
+    ]
+    for c in started:
+        c.start()
     lines = []
     for k, weight in enumerate((w_key, w_key_two)):
         high, low = split2(grads[k * HEADS : (k + 1) * HEADS])
@@ -328,7 +333,7 @@
 
 
 def token_kernel(value_grad, score_grad, w_value, fold_one, out):
-    grad = nt(value_grad[...], w_value[...]) + folded_back(score_grad[...], fold_one[...])
+    grad = nt(value_grad[...], w_value[...]) + folded_back(score_grad[...].T, fold_one[...])
     out[...] = grad.astype(BF16).reshape(CH, BLK, D)
 
 
@@ -456,7 +461,7 @@
         back_kernel,
         (
             shape((NB * TOK, D), BF16),
-            shape((NB * TOK, HEADS), F32),
+            shape((HEADS, NB * TOK), F32),
             shape((16, SLAB, 512), BF16),
             shape((8, 8, 512), F32),
         ),
@@ -470,6 +475,7 @@
             pltpu.VMEM((NB * TOK, D), BF16),
             pltpu.VMEM((16, SLAB, 512), BF16),
             pltpu.VMEM((NB * TOK, HEADS), F32),
+            pltpu.VMEM((HEADS, NB * TOK), F32),
             pltpu.VMEM((8, 8, 512), F32),
             pltpu.SemaphoreType.DMA((14,)),
         ],
@@ -509,7 +515,12 @@
         6 * 10**6,
         24,
         grid=(NB,),
-        in_specs=[by_rows(TOK, D), by_rows(TOK, HEADS), full, whole((D, 3 * HEADS))],
+        in_specs=[
+            by_rows(TOK, D),
+            pl.BlockSpec((HEADS, TOK), lambda i: (0, i)),
+            full,
+            whole((D, 3 * HEADS)),
+        ],
         out_specs=token_spec,
     )(value_grad, score_grad, w_value, fold_one)
     rows = call(rows_kernel, shape((8, 8, D), BF16), 10**6, 2 * 10**6, 8)(got)

time: 117 us -> 117 us (level)
    unnamed x18 -> x16, local copies, waits for them, and re-layouts: 3.02 us -> 3.01 us
where the time goes in v5:
time: 117 us; the launch traced here: 116 us
  Pallas kernels  35.8 us (31%)
  blocking collectives  34.5 us (29%)
  waiting for transfers between devices  23.6 us (20%)
  starting transfers between devices  17.5 us (15%)
  local copies, waits for them, and re-layouts  3.86 us (3%)
    all_to_all x1, blocking collectives, shards(): lax.all_to_all(pairs, ('chan', 'patch'), 0, 0, tiled=True, axis_index_gro...  22.8 us
    pallas_call x1, Pallas kernels, shards(): call(forward_kernel, (shape((NB * TOK, D), F32), shape((NB * TOK, HEADS),...  12 us
    all_to_all x1, waiting for transfers between devices, shards(): stats = lax.all_to_all(stats, 'chan', 0, 0, tiled=True)  12 us
    all_to_all x1, blocking collectives, shards(): lax.all_to_all(rows, 'chan', 0, 0, tiled=True, axis_index_groups=same_half)  11.7 us
    all_to_all x1, starting transfers between devices, shards(): cot = lax.all_to_all(tiled, 'chan', 0, 0, tiled=True).reshape(ROWS, D)  10.3 us
    pallas_call x1, Pallas kernels, shards(): call(back_kernel, (shape((NB * TOK, D), BF16), shape((HEADS, NB * TOK), F...  7.54 us
    all_to_all x1, waiting for transfers between devices, shards(): cot = lax.all_to_all(tiled, 'chan', 0, 0, tiled=True).reshape(ROWS, D)  6.65 us
    all_to_all x1, waiting for transfers between devices, shards(): rows = lax.all_to_all(rows, 'chan', 0, 0, tiled=True)  4.33 us
  transfers between devices with their start and end apart: 4, of which 4 were waited for; matrix products, arithmetic and copies ran while one was open for 0% of the time, Pallas kernels for 19%

profile of v5, /device:TPU:8, one launch (start us, length us, event | category | flops | bytes accessed | tf_op | source)
XLA Modules:
  0.0 116.0 jit_solution(9779217544762946760)
XLA Ops:
  0.6 1.6 %shard_map.128 = bf16[16,12,1024]{2,1,0:T(8,128)(2,1)} custom-call(bf16[1,12,1024]{2,1,0:T(8,128)(2,1)} %cot.1), custom_call_target="tpu_custom_call" | custom-call | flops 10000 | bytes 1000000 | tf_op jit(solution)/shard_map/pallas_call | solution.py:405
  2.3 10.3 %all-to-all-start = ((bf16[16,12,1024]{2,1,0:T(8,128)(2,1)}), bf16[16,12,1024]{2,1,0:T(8,128)(2,1)S(1)}, u32[]{:S(2)}, u32[]{:S(2)}) async-start(bf16[16,12,1024]{2,1,0:T(8,128)(2,1)} %shard_map.128), calls=%async_computation | async-start | bytes 1048576 | tf_op jit(solution)/shard_map/all_to_all | solution.py:411
  12.6 12.0 %shard_map.127 = (f32[768,1024]{1,0:T(8,128)}, f32[768,16]{1,0:T(8,128)}, bf16[384,1024]{1,0:T(8,128)(2,1)}, bf16[1024,384]{1,0:T(8,128)(2,1)}, bf16[1024,768]{1...) custom-call(s32[4]{0:T(128)} %table.3, ...), custom_call_target="tpu_custom_call" | custom-call | flops 4000000000 | bytes 16000000 | tf_op jit(solution)/shard_map/pallas_call | solution.py:416
  24.6 6.6 %all-to-all-done = bf16[16,12,1024]{2,1,0:T(8,128)(2,1)S(1)} async-done(((bf16[16,12,1024]{2,1,0:T(8,128)(2,1)}), bf16[16,12,1024]{2,1,0:T(8,128)(2,1)S(1)}, u32[]{:S(2)}, u32[]{:S(2)}) %all-to-all-start) | async-done | bytes 393248 | tf_op jit(solution)/shard_map/all_to_all | solution.py:411
  31.2 0.8 reshape.33.cot.cot_h
  32.1 2.8 %shard_map.129 = (f32[384,32]{1,0:T(8,128)}, f32[16,48,128]{2,1,0:T(8,128)}) custom-call(bf16[384,1024]{1,0:T(8,128)(2,1)} %get-tuple-element.30.agg, bf16[192,1024]{1,0:T(8,128)(2,1)} %reshape.33.cot.cot_h, f32[384,16]{1,0:T(8,128)} %get-tuple-element.31.scores_two), custom_call_target="tpu_custom_call" | custom-call | flops 1000000000 | bytes 2000000 | tf_op jit(solution)/shard_map/pallas_call | solution.py:446
  34.9 3.6 %all-to-all-start.1 = ((f32[16,48,128]{2,1,0:T(8,128)}), f32[16,48,128]{2,1,0:T(8,128)S(1)}, u32[]{:S(2)}, u32[]{:S(2)}) async-start(f32[16,48,128]{2,1,0:T(8,128)} %get-tuple-element.35), calls=%async_computation.1 | async-start | bytes 786432 | tf_op jit(solution)/shard_map/all_to_all | solution.py:453
  38.4 0.0 copy-start.6
  38.4 3.9 %shard_map.131.weights_h = f32[768,32]{1,0:T(8,128)} custom-call(f32[768,1024]{1,0:T(8,128)} %get-tuple-element.37.values, bf16[192,1024]{1,0:T(8,128)(2,1)} %reshape.33.cot.cot_h, f32[768,16]{1,0:T(8,128)} %get-tuple-element.38.weights), custom_call_target="tpu_custom_call" | custom-call | flops 1000000000 | bytes 5000000 | tf_op jit(solution)/shard_map/pallas_call | solution.py:455
  42.3 12.0 %all-to-all-done.1.stats = f32[16,48,128]{2,1,0:T(8,128)S(1)} async-done(((f32[16,48,128]{2,1,0:T(8,128)}), f32[16,48,128]{2,1,0:T(8,128)S(1)}, u32[]{:S(2)}, u32[]{:S(2)}) %all-to-all-start.1) | async-done | bytes 393248 | tf_op jit(solution)/shard_map/all_to_all | solution.py:453
  54.2 0.1 shard_map.130.totals_h
  54.3 0.0 copy-done.6
  54.3 0.0 copy-start
  54.3 7.5 %shard_map.132 = (bf16[768,1024]{1,0:T(8,128)(2,1)}, f32[16,768]{1,0:T(8,128)S(1)}, bf16[16,72,512]{2,1,0:T(8,128)(2,1)}, f32[8,8,512]{2,1,0:T(8,128)S(1)}) custom-call(s32[4]{0:T(128)S(1)} %copy-done.6, s32[1]{0:T(128)} %bitcast.core, f32[48,128]{1,0:T(8,128)S(1)} %shard_map.130.totals_h, bf16[192,1024]{1,0:T(8,128)(2,1)} %reshape.33.cot.cot_h, ...), custom_call_target="tpu_custom_call" | custom-call | flops 4000000000 | bytes 16000000 | tf_op jit(solution)/shard_map/pallas_call | solution.py:460
  61.9 0.1 collective-permute-start
  62.0 0.0 copy-done
  62.0 0.0 copy-start.1
  62.0 1.4 %copy-done.1 = bf16[768,1024]{1,0:T(8,128)(2,1)S(1)} copy-done((bf16[768,1024]{1,0:T(8,128)(2,1)S(1)}, bf16[768,1024]{1,0:T(8,128)(2,1)}, u32[]{:S(2)}) %copy-start.1) | copy-done | bytes 1572888
  63.4 1.0 shard_map.134.keep
  64.4 0.6 collective-permute-done.got
  65.0 0.3 shard_map.135
  65.3 22.8 %all_to_all.25.got = bf16[16,72,512]{2,1,0:T(8,128)(2,1)S(1)} all-to-all(bf16[16,72,512]{2,1,0:T(8,128)(2,1)S(1)} %shard_map.135), channel_id=1, replica_groups={{0,2,4,6,8,10,12,14,16,18,20,22,24,26,28,30},{1,3,5,7,9,11,13,15,17,19,..., dimensions={0} | all-to-all | bytes 2359296 | tf_op jit(solution)/shard_map/all_to_all | solution.py:508
  88.0 0.0 copy-start.2
  88.1 0.0 copy-start.7
  88.1 0.2 shard_map.136
  88.2 11.7 %all_to_all.26.got = bf16[8,8,1024]{2,1,0:T(8,128)(2,1)S(1)} all-to-all(bf16[8,8,1024]{2,1,0:T(8,128)(2,1)S(1)} %shard_map.136), channel_id=1, replica_groups={{0,32,64,96,128,160,192,224},{16,48,80,112,144,176,208,240},{1,33,65,97..., dimensions={0} | all-to-all | bytes 262144 | tf_op jit(solution)/shard_map/all_to_all | solution.py:528
  99.9 0.7 shard_map.137
  100.6 3.5 %all-to-all-start.4 = ((bf16[16,8,512]{2,1,0:T(8,128)(2,1)}), bf16[16,8,512]{2,1,0:T(8,128)(2,1)S(1)}, u32[]{:S(2)}, u32[]{:S(2)}) async-start(bf16[16,8,512]{2,1,0:T(8,128)(2,1)} %get-tuple-element.50), calls=%async_computation.4 | async-start | bytes 262144 | tf_op jit(solution)/shard_map/all_to_all | solution.py:532
  104.1 0.0 copy-done.2
  104.1 0.0 copy-done.7
  104.2 0.0 copy-start.3
  104.2 1.6 %copy-done.3 = bf16[1024,1024]{1,0:T(8,128)(2,1)S(1)} copy-done((bf16[1024,1024]{1,0:T(8,128)(2,1)S(1)}, bf16[1024,1024]{1,0:T(8,128)(2,1)}, u32[]{:S(2)}) %copy-start.3) | copy-done | bytes 2097176
  105.8 0.0 copy-start.4
  105.8 0.0 copy-start.5
  105.8 4.0 %shard_map.133 = bf16[4,192,1024]{2,1,0:T(8,128)(2,1)} custom-call(bf16[768,1024]{1,0:T(8,128)(2,1)S(1)} %copy-done.2, f32[16,768]{1,0:T(8,128)S(1)} %get-tuple-element.44.score_grad, bf16[1024,1024]{1,0:T(8,128)(2,1)S(1)} %copy-done.3, bf16[1024,48]{1,0:T(8,128)(2,1)S(1)} %copy-done.7), custom_call_target="tpu_custom_call" | custom-call | flops 2000000000 | bytes 6000000 | tf_op jit(solution)/shard_map/pallas_call | solution.py:511
  109.8 0.0 copy-done.4
  109.8 0.0 copy-done.5
  109.8 1.2 shard_map.138
  111.0 4.3 %all-to-all-done.4.got = bf16[16,8,512]{2,1,0:T(8,128)(2,1)S(1)} async-done(((bf16[16,8,512]{2,1,0:T(8,128)(2,1)}), bf16[16,8,512]{2,1,0:T(8,128)(2,1)S(1)}, u32[]{:S(2)}, u32[]{:S(2)}) %all-to-all-start.4) | async-done | bytes 131104 | tf_op jit(solution)/shard_map/all_to_all | solution.py:532
  115.3 0.7 shard_map.139
Async XLA Ops:
  2.3 29.0 %all-to-all-start = ((bf16[16,12,1024]{2,1,0:T(8,128)(2,1)}), bf16[16,12,1024]{2,1,0:T(8,128)(2,1)S(1)}, u32[]{:S(2)}, u32[]{:S(2)}) async-start(bf16[16,12,1024]{2,1,0:T(8,128)(2,1)} %shard_map.128), calls=%async_computation | async-start | bytes 1048576 | tf_op jit(solution)/shard_map/all_to_all | solution.py:411
  34.9 19.4 %all-to-all-start.1 = ((f32[16,48,128]{2,1,0:T(8,128)}), f32[16,48,128]{2,1,0:T(8,128)S(1)}, u32[]{:S(2)}, u32[]{:S(2)}) async-start(f32[16,48,128]{2,1,0:T(8,128)} %get-tuple-element.35), calls=%async_computation.1 | async-start | bytes 786432 | tf_op jit(solution)/shard_map/all_to_all | solution.py:453
  38.4 15.9 %copy-start.6 = (s32[4]{0:T(128)S(1)}, s32[4]{0:T(128)}, u32[]{:S(2)}) copy-start(s32[4]{0:T(128)} %table.3) | copy-start | bytes 52
  54.3 7.7 %copy-start = (bf16[1024,768]{1,0:T(8,128)(2,1)S(1)}, bf16[1024,768]{1,0:T(8,128)(2,1)}, u32[]{:S(2)}) copy-start(bf16[1024,768]{1,0:T(8,128)(2,1)} %get-tuple-element.40.tok_h.tok_t) | copy-start | bytes 4718596
  61.9 3.1 %collective-permute-start = (bf16[16,72,512]{2,1,0:T(8,128)(2,1)}, bf16[16,72,512]{2,1,0:T(8,128)(2,1)S(1)}, u32[]{:S(2)}, u32[]{:S(2)}) collective-permute-start(bf16[16,72,512]{2,1,0:T(8,128)(2,1)} %get-tuple-element.47), channel_id=1, source_target_pairs={{0,1},{1,0},{2,3},{3,2},{4,5},{5,4},{6,7},{7,6},{8,9},{9,8},{10,11... | collective-permute-start | bytes 3538952 | tf_op jit(solution)/shard_map/ppermute | solution.py:483
  62.0 1.4 %copy-start.1 = (bf16[768,1024]{1,0:T(8,128)(2,1)S(1)}, bf16[768,1024]{1,0:T(8,128)(2,1)}, u32[]{:S(2)}) copy-start(bf16[768,1024]{1,0:T(8,128)(2,1)} %get-tuple-element.43.value_grad) | copy-start | bytes 4718596
  88.0 16.1 %copy-start.2 = (bf16[768,1024]{1,0:T(8,128)(2,1)S(1)}, bf16[768,1024]{1,0:T(8,128)(2,1)}, u32[]{:S(2)}) copy-start(bf16[768,1024]{1,0:T(8,128)(2,1)} %get-tuple-element.43.value_grad) | copy-start | bytes 4718596
  88.1 16.1 %copy-start.7 = (bf16[1024,48]{1,0:T(8,128)(2,1)S(1)}, bf16[1024,48]{1,0:T(8,128)(2,1)}, u32[]{:S(2)}) copy-start(bf16[1024,48]{1,0:T(8,128)(2,1)} %get-tuple-element.45.fold_one) | copy-start | bytes 294916
  100.6 14.7 %all-to-all-start.4 = ((bf16[16,8,512]{2,1,0:T(8,128)(2,1)}), bf16[16,8,512]{2,1,0:T(8,128)(2,1)S(1)}, u32[]{:S(2)}, u32[]{:S(2)}) async-start(bf16[16,8,512]{2,1,0:T(8,128)(2,1)} %get-tuple-element.50), calls=%async_computation.4 | async-start | bytes 262144 | tf_op jit(solution)/shard_map/all_to_all | solution.py:532
  104.2 1.6 %copy-start.3 = (bf16[1024,1024]{1,0:T(8,128)(2,1)S(1)}, bf16[1024,1024]{1,0:T(8,128)(2,1)}, u32[]{:S(2)}) copy-start(bf16[1024,1024]{1,0:T(8,128)(2,1)} %w_value.3) | copy-start | bytes 6291460
  105.8 4.1 %copy-start.4 = (f32[1024]{0:T(1024)S(1)}, f32[1024]{0:T(1024)}, u32[]{:S(2)}) copy-start(f32[1024]{0:T(1024)} %param.12) | copy-start | bytes 12292
  105.8 4.1 %copy-start.5 = (f32[1024]{0:T(1024)S(1)}, f32[1024]{0:T(1024)}, u32[]{:S(2)}) copy-start(f32[1024]{0:T(1024)} %param.14) | copy-start | bytes 12292

commit v6 on v5

--- a/solution.py
+++ b/solution.py
@@ -341,9 +341,8 @@
     total = got[0].astype(F32)
     for k in range(1, 16):
         total = total + got[k].astype(F32)
-    total = total.astype(BF16)
     for z in range(8):
-        out[z] = jnp.concatenate([total[8 * z : 8 * z + 8], total[64:]], 1)
+        out[z] = jnp.concatenate([total[8 * z : 8 * z + 8], total[64:]], 1).astype(BF16)
 
 
 def chans_kernel(got, rows, extra):

time: 117 us -> 117 us (level)
  no operation moved by 1% of the time
where the time goes in v6:
time: 117 us; the launch traced here: 116 us
  Pallas kernels  35.8 us (31%)
  blocking collectives  34.5 us (29%)
  waiting for transfers between devices  23.6 us (20%)
  starting transfers between devices  17.5 us (15%)
  local copies, waits for them, and re-layouts  3.86 us (3%)
    all_to_all x1, blocking collectives, shards(): lax.all_to_all(pairs, ('chan', 'patch'), 0, 0, tiled=True, axis_index_gro...  22.8 us
    pallas_call x1, Pallas kernels, shards(): call(forward_kernel, (shape((NB * TOK, D), F32), shape((NB * TOK, HEADS),...  12 us
    all_to_all x1, waiting for transfers between devices, shards(): stats = lax.all_to_all(stats, 'chan', 0, 0, tiled=True)  12 us
    all_to_all x1, blocking collectives, shards(): lax.all_to_all(rows, 'chan', 0, 0, tiled=True, axis_index_groups=same_half)  11.7 us
    all_to_all x1, starting transfers between devices, shards(): cot = lax.all_to_all(tiled, 'chan', 0, 0, tiled=True).reshape(ROWS, D)  10.3 us
    pallas_call x1, Pallas kernels, shards(): call(back_kernel, (shape((NB * TOK, D), BF16), shape((HEADS, NB * TOK), F...  7.54 us
    all_to_all x1, waiting for transfers between devices, shards(): cot = lax.all_to_all(tiled, 'chan', 0, 0, tiled=True).reshape(ROWS, D)  6.65 us
    all_to_all x1, waiting for transfers between devices, shards(): rows = lax.all_to_all(rows, 'chan', 0, 0, tiled=True)  4.33 us
  transfers between devices with their start and end apart: 4, of which 4 were waited for; matrix products, arithmetic and copies ran while one was open for 0% of the time, Pallas kernels for 19%

profile of v6, /device:TPU:8, one launch (start us, length us, event | category | flops | bytes accessed | tf_op | source)
XLA Modules:
  0.0 116.0 jit_solution(9779217544762946760)
XLA Ops:
  0.6 1.6 %shard_map.128 = bf16[16,12,1024]{2,1,0:T(8,128)(2,1)} custom-call(bf16[1,12,1024]{2,1,0:T(8,128)(2,1)} %cot.1), custom_call_target="tpu_custom_call" | custom-call | flops 10000 | bytes 1000000 | tf_op jit(solution)/shard_map/pallas_call | solution.py:404
  2.3 10.3 %all-to-all-start = ((bf16[16,12,1024]{2,1,0:T(8,128)(2,1)}), bf16[16,12,1024]{2,1,0:T(8,128)(2,1)S(1)}, u32[]{:S(2)}, u32[]{:S(2)}) async-start(bf16[16,12,1024]{2,1,0:T(8,128)(2,1)} %shard_map.128), calls=%async_computation | async-start | bytes 1048576 | tf_op jit(solution)/shard_map/all_to_all | solution.py:410
  12.6 12.0 %shard_map.127 = (f32[768,1024]{1,0:T(8,128)}, f32[768,16]{1,0:T(8,128)}, bf16[384,1024]{1,0:T(8,128)(2,1)}, bf16[1024,384]{1,0:T(8,128)(2,1)}, bf16[1024,768]{1...) custom-call(s32[4]{0:T(128)} %table.3, ...), custom_call_target="tpu_custom_call" | custom-call | flops 4000000000 | bytes 16000000 | tf_op jit(solution)/shard_map/pallas_call | solution.py:415
  24.6 6.6 %all-to-all-done = bf16[16,12,1024]{2,1,0:T(8,128)(2,1)S(1)} async-done(((bf16[16,12,1024]{2,1,0:T(8,128)(2,1)}), bf16[16,12,1024]{2,1,0:T(8,128)(2,1)S(1)}, u32[]{:S(2)}, u32[]{:S(2)}) %all-to-all-start) | async-done | bytes 393248 | tf_op jit(solution)/shard_map/all_to_all | solution.py:410
  31.2 0.8 reshape.33.cot.cot_h
  32.1 2.8 %shard_map.129 = (f32[384,32]{1,0:T(8,128)}, f32[16,48,128]{2,1,0:T(8,128)}) custom-call(bf16[384,1024]{1,0:T(8,128)(2,1)} %get-tuple-element.30.agg, bf16[192,1024]{1,0:T(8,128)(2,1)} %reshape.33.cot.cot_h, f32[384,16]{1,0:T(8,128)} %get-tuple-element.31.scores_two), custom_call_target="tpu_custom_call" | custom-call | flops 1000000000 | bytes 2000000 | tf_op jit(solution)/shard_map/pallas_call | solution.py:445
  34.9 3.6 %all-to-all-start.1 = ((f32[16,48,128]{2,1,0:T(8,128)}), f32[16,48,128]{2,1,0:T(8,128)S(1)}, u32[]{:S(2)}, u32[]{:S(2)}) async-start(f32[16,48,128]{2,1,0:T(8,128)} %get-tuple-element.35), calls=%async_computation.1 | async-start | bytes 786432 | tf_op jit(solution)/shard_map/all_to_all | solution.py:452
  38.4 0.0 copy-start.6
  38.4 3.9 %shard_map.131.weights_h = f32[768,32]{1,0:T(8,128)} custom-call(f32[768,1024]{1,0:T(8,128)} %get-tuple-element.37.values, bf16[192,1024]{1,0:T(8,128)(2,1)} %reshape.33.cot.cot_h, f32[768,16]{1,0:T(8,128)} %get-tuple-element.38.weights), custom_call_target="tpu_custom_call" | custom-call | flops 1000000000 | bytes 5000000 | tf_op jit(solution)/shard_map/pallas_call | solution.py:454
  42.3 12.0 %all-to-all-done.1.stats = f32[16,48,128]{2,1,0:T(8,128)S(1)} async-done(((f32[16,48,128]{2,1,0:T(8,128)}), f32[16,48,128]{2,1,0:T(8,128)S(1)}, u32[]{:S(2)}, u32[]{:S(2)}) %all-to-all-start.1) | async-done | bytes 393248 | tf_op jit(solution)/shard_map/all_to_all | solution.py:452
  54.2 0.1 shard_map.130.totals_h
  54.3 0.0 copy-done.6
  54.3 0.0 copy-start
  54.3 7.5 %shard_map.132 = (bf16[768,1024]{1,0:T(8,128)(2,1)}, f32[16,768]{1,0:T(8,128)S(1)}, bf16[16,72,512]{2,1,0:T(8,128)(2,1)}, f32[8,8,512]{2,1,0:T(8,128)S(1)}) custom-call(s32[4]{0:T(128)S(1)} %copy-done.6, s32[1]{0:T(128)} %bitcast.core, f32[48,128]{1,0:T(8,128)S(1)} %shard_map.130.totals_h, bf16[192,1024]{1,0:T(8,128)(2,1)} %reshape.33.cot.cot_h, ...), custom_call_target="tpu_custom_call" | custom-call | flops 4000000000 | bytes 16000000 | tf_op jit(solution)/shard_map/pallas_call | solution.py:459
  61.9 0.1 collective-permute-start
  62.0 0.0 copy-done
  62.0 0.0 copy-start.1
  62.0 1.4 %copy-done.1 = bf16[768,1024]{1,0:T(8,128)(2,1)S(1)} copy-done((bf16[768,1024]{1,0:T(8,128)(2,1)S(1)}, bf16[768,1024]{1,0:T(8,128)(2,1)}, u32[]{:S(2)}) %copy-start.1) | copy-done | bytes 1572888
  63.4 1.0 shard_map.134.keep
  64.4 0.6 collective-permute-done.got
  65.0 0.3 shard_map.135
  65.3 22.8 %all_to_all.25.got = bf16[16,72,512]{2,1,0:T(8,128)(2,1)S(1)} all-to-all(bf16[16,72,512]{2,1,0:T(8,128)(2,1)S(1)} %shard_map.135), channel_id=1, replica_groups={{0,2,4,6,8,10,12,14,16,18,20,22,24,26,28,30},{1,3,5,7,9,11,13,15,17,19,..., dimensions={0} | all-to-all | bytes 2359296 | tf_op jit(solution)/shard_map/all_to_all | solution.py:507
  88.0 0.0 copy-start.2
  88.1 0.0 copy-start.7
  88.1 0.2 shard_map.136
  88.2 11.7 %all_to_all.26.got = bf16[8,8,1024]{2,1,0:T(8,128)(2,1)S(1)} all-to-all(bf16[8,8,1024]{2,1,0:T(8,128)(2,1)S(1)} %shard_map.136), channel_id=1, replica_groups={{0,32,64,96,128,160,192,224},{16,48,80,112,144,176,208,240},{1,33,65,97..., dimensions={0} | all-to-all | bytes 262144 | tf_op jit(solution)/shard_map/all_to_all | solution.py:527
  99.9 0.7 shard_map.137
  100.6 3.5 %all-to-all-start.4 = ((bf16[16,8,512]{2,1,0:T(8,128)(2,1)}), bf16[16,8,512]{2,1,0:T(8,128)(2,1)S(1)}, u32[]{:S(2)}, u32[]{:S(2)}) async-start(bf16[16,8,512]{2,1,0:T(8,128)(2,1)} %get-tuple-element.50), calls=%async_computation.4 | async-start | bytes 262144 | tf_op jit(solution)/shard_map/all_to_all | solution.py:531
  104.1 0.0 copy-done.2
  104.1 0.0 copy-done.7
  104.2 0.0 copy-start.3
  104.2 1.6 %copy-done.3 = bf16[1024,1024]{1,0:T(8,128)(2,1)S(1)} copy-done((bf16[1024,1024]{1,0:T(8,128)(2,1)S(1)}, bf16[1024,1024]{1,0:T(8,128)(2,1)}, u32[]{:S(2)}) %copy-start.3) | copy-done | bytes 2097176
  105.8 0.0 copy-start.4
  105.8 0.0 copy-start.5
  105.8 4.0 %shard_map.133 = bf16[4,192,1024]{2,1,0:T(8,128)(2,1)} custom-call(bf16[768,1024]{1,0:T(8,128)(2,1)S(1)} %copy-done.2, f32[16,768]{1,0:T(8,128)S(1)} %get-tuple-element.44.score_grad, bf16[1024,1024]{1,0:T(8,128)(2,1)S(1)} %copy-done.3, bf16[1024,48]{1,0:T(8,128)(2,1)S(1)} %copy-done.7), custom_call_target="tpu_custom_call" | custom-call | flops 2000000000 | bytes 6000000 | tf_op jit(solution)/shard_map/pallas_call | solution.py:510
  109.8 0.0 copy-done.4
  109.8 0.0 copy-done.5
  109.8 1.2 shard_map.138
  111.0 4.3 %all-to-all-done.4.got = bf16[16,8,512]{2,1,0:T(8,128)(2,1)S(1)} async-done(((bf16[16,8,512]{2,1,0:T(8,128)(2,1)}), bf16[16,8,512]{2,1,0:T(8,128)(2,1)S(1)}, u32[]{:S(2)}, u32[]{:S(2)}) %all-to-all-start.4) | async-done | bytes 131104 | tf_op jit(solution)/shard_map/all_to_all | solution.py:531
  115.3 0.7 shard_map.139
Async XLA Ops:
  2.3 29.0 %all-to-all-start = ((bf16[16,12,1024]{2,1,0:T(8,128)(2,1)}), bf16[16,12,1024]{2,1,0:T(8,128)(2,1)S(1)}, u32[]{:S(2)}, u32[]{:S(2)}) async-start(bf16[16,12,1024]{2,1,0:T(8,128)(2,1)} %shard_map.128), calls=%async_computation | async-start | bytes 1048576 | tf_op jit(solution)/shard_map/all_to_all | solution.py:410
  34.9 19.4 %all-to-all-start.1 = ((f32[16,48,128]{2,1,0:T(8,128)}), f32[16,48,128]{2,1,0:T(8,128)S(1)}, u32[]{:S(2)}, u32[]{:S(2)}) async-start(f32[16,48,128]{2,1,0:T(8,128)} %get-tuple-element.35), calls=%async_computation.1 | async-start | bytes 786432 | tf_op jit(solution)/shard_map/all_to_all | solution.py:452
  38.4 15.9 %copy-start.6 = (s32[4]{0:T(128)S(1)}, s32[4]{0:T(128)}, u32[]{:S(2)}) copy-start(s32[4]{0:T(128)} %table.3) | copy-start | bytes 52
  54.3 7.7 %copy-start = (bf16[1024,768]{1,0:T(8,128)(2,1)S(1)}, bf16[1024,768]{1,0:T(8,128)(2,1)}, u32[]{:S(2)}) copy-start(bf16[1024,768]{1,0:T(8,128)(2,1)} %get-tuple-element.40.tok_h.tok_t) | copy-start | bytes 4718596
  61.9 3.1 %collective-permute-start = (bf16[16,72,512]{2,1,0:T(8,128)(2,1)}, bf16[16,72,512]{2,1,0:T(8,128)(2,1)S(1)}, u32[]{:S(2)}, u32[]{:S(2)}) collective-permute-start(bf16[16,72,512]{2,1,0:T(8,128)(2,1)} %get-tuple-element.47), channel_id=1, source_target_pairs={{0,1},{1,0},{2,3},{3,2},{4,5},{5,4},{6,7},{7,6},{8,9},{9,8},{10,11... | collective-permute-start | bytes 3538952 | tf_op jit(solution)/shard_map/ppermute | solution.py:482
  62.0 1.4 %copy-start.1 = (bf16[768,1024]{1,0:T(8,128)(2,1)S(1)}, bf16[768,1024]{1,0:T(8,128)(2,1)}, u32[]{:S(2)}) copy-start(bf16[768,1024]{1,0:T(8,128)(2,1)} %get-tuple-element.43.value_grad) | copy-start | bytes 4718596
  88.0 16.1 %copy-start.2 = (bf16[768,1024]{1,0:T(8,128)(2,1)S(1)}, bf16[768,1024]{1,0:T(8,128)(2,1)}, u32[]{:S(2)}) copy-start(bf16[768,1024]{1,0:T(8,128)(2,1)} %get-tuple-element.43.value_grad) | copy-start | bytes 4718596
  88.1 16.1 %copy-start.7 = (bf16[1024,48]{1,0:T(8,128)(2,1)S(1)}, bf16[1024,48]{1,0:T(8,128)(2,1)}, u32[]{:S(2)}) copy-start(bf16[1024,48]{1,0:T(8,128)(2,1)} %get-tuple-element.45.fold_one) | copy-start | bytes 294916
  100.6 14.7 %all-to-all-start.4 = ((bf16[16,8,512]{2,1,0:T(8,128)(2,1)}), bf16[16,8,512]{2,1,0:T(8,128)(2,1)S(1)}, u32[]{:S(2)}, u32[]{:S(2)}) async-start(bf16[16,8,512]{2,1,0:T(8,128)(2,1)} %get-tuple-element.50), calls=%async_computation.4 | async-start | bytes 262144 | tf_op jit(solution)/shard_map/all_to_all | solution.py:531
  104.2 1.6 %copy-start.3 = (bf16[1024,1024]{1,0:T(8,128)(2,1)S(1)}, bf16[1024,1024]{1,0:T(8,128)(2,1)}, u32[]{:S(2)}) copy-start(bf16[1024,1024]{1,0:T(8,128)(2,1)} %w_value.3) | copy-start | bytes 6291460
  105.8 4.1 %copy-start.4 = (f32[1024]{0:T(1024)S(1)}, f32[1024]{0:T(1024)}, u32[]{:S(2)}) copy-start(f32[1024]{0:T(1024)} %param.12) | copy-start | bytes 12292
  105.8 4.1 %copy-start.5 = (f32[1024]{0:T(1024)S(1)}, f32[1024]{0:T(1024)}, u32[]{:S(2)}) copy-start(f32[1024]{0:T(1024)} %param.14) | copy-start | bytes 12292
